TPU v7x, 32 devices: a whole 2x2x4 slice. The times are simulated.
32 devices in a mesh: tm: 8 (over z, y), grp: 4 (over x, core).
Axes of the slice: x: 2, y: 2, z: 4, core: 2. Of those that a mesh axis runs over, the one named last changes fastest.
Arguments:
- voltages: bfloat16 [1, 24, 2, 2, 262144], P(None, None, None, None, ('tm', 'grp')), may hold values from -8 to 8
- chirp_phase: float32 [24, 512, 512], P(None, 'tm'), may hold values from -3.140625 to 3.140625
- intersection: int32 [24], replicated, may hold values from 1 to 131072
- group_of: int32 [24], replicated, may hold values from 0 to 3, as said below
Outputs:
- group_power: float32 [1, 4, 131072], P(None, None, ('tm', 'grp'))
Inputs may be any that keep to these rules, and one draw needn't show every extreme that they name: `group_of`: every one of the 4 groups holds at least one channel and at most 12; some group holds exactly 12.
All inputs are finite; a program needn't handle non-finite values.
Results may differ from a plain program's by a relative error of at most 0.0003.
Values may be sent and summed in bfloat16 or wider, within the bound.
A program may use at most 128 MiB of HBM per device.

v0:
```python
import math

import jax
import jax.numpy as jnp
from jax import lax
from jax.sharding import PartitionSpec as P

NFFT = 262144
F1 = 512
F2 = 512


full_turn = 2.0 * math.pi
highest = lax.Precision.HIGHEST


def turn_angle(product, period):
    return full_turn * (product % period).astype(jnp.float32) / period


def on_device(voltages, chirp_phase, intersection, group_of):
    tm_count = lax.axis_size("tm")
    grp_count = lax.axis_size("grp")
    tm_rank = lax.axis_index("tm")
    grp_rank = lax.axis_index("grp")
    beams = voltages.shape[0]
    chans = voltages.shape[1]
    pols = voltages.shape[2]
    local_len = voltages.shape[4]
    a_rows = local_len // F2
    q_cols = F2 // tm_count
    k_cols = F1 // tm_count
    half_rows = F1 // 2
    group_ids = jnp.arange(grp_count, dtype=jnp.int32)
    member = (group_of[None, :] == group_ids[:, None]).astype(jnp.int32)
    counts = jnp.sum(member, axis=1)
    slot_table = jnp.arange(chans, dtype=jnp.int32).reshape(grp_count, chans // grp_count)
    own_slots = slot_table[grp_rank]
    weights = (
        jnp.transpose(member[:, own_slots]).astype(jnp.float32)
        / (2.0 * counts.astype(jnp.float32))[None, :]
    )
    slots = own_slots.shape[0]
    picked = jnp.take(voltages, slot_table, axis=1).reshape(
        beams, grp_count, slots, pols, 2, a_rows, tm_count, q_cols
    )
    outgoing = jnp.transpose(picked, (0, 1, 2, 3, 4, 6, 7, 5))
    arrived = lax.all_to_all(
        lax.all_to_all(outgoing, "tm", split_axis=5, concat_axis=7, tiled=True),
        "grp",
        split_axis=1,
        concat_axis=1,
        tiled=True,
    )
    arrived = arrived[:, :, :, :, :, 0].astype(jnp.float32)
    row_ids = jnp.arange(a_rows * tm_count, dtype=jnp.int32)
    a_index = (
        a_rows * grp_count * (row_ids // a_rows)[None, :]
        + a_rows * group_ids[:, None]
        + (row_ids % a_rows)[None, :]
    )
    freq_first = jnp.arange(F1, dtype=jnp.int32)
    angle_one = turn_angle(a_index[:, :, None] * freq_first[None, None, :], F1)
    first_cos = jnp.einsum("bgspiqr,grz->bspizq", arrived, jnp.cos(angle_one), precision=highest)
    first_sin = jnp.einsum("bgspiqr,grz->bspizq", arrived, jnp.sin(angle_one), precision=highest)
    real_first = first_cos[:, :, :, 0] + first_sin[:, :, :, 1]
    imag_first = first_cos[:, :, :, 1] - first_sin[:, :, :, 0]
    b_index = tm_rank * q_cols + jnp.arange(q_cols, dtype=jnp.int32)
    first_twist = turn_angle(freq_first[:, None] * b_index[None, :], NFFT)
    twist_one_cos = jnp.cos(first_twist)
    twist_one_sin = jnp.sin(first_twist)
    section = jnp.stack(
        [
            real_first * twist_one_cos + imag_first * twist_one_sin,
            imag_first * twist_one_cos - real_first * twist_one_sin,
        ],
        axis=3,
    )
    section = section.reshape(beams, slots, pols, 2, tm_count, k_cols, q_cols)
    k1_index = tm_rank * k_cols + jnp.arange(k_cols, dtype=jnp.int32)
    k2_index = jnp.arange(F2, dtype=jnp.int32)
    shifts = intersection[own_slots]
    ramp = (
        k1_index[None, :, None] * shifts[:, None, None]
        + F1 * (k2_index[None, None, :] * shifts[:, None, None] % F2)
    ) % NFFT
    phase_total = (
        jnp.take(chirp_phase, own_slots, axis=0) + full_turn * ramp.astype(jnp.float32) / NFFT
    )
    chirp_cos = (jnp.cos(phase_total) / NFFT)[:, None]
    chirp_sin = (jnp.sin(phase_total) / NFFT)[:, None]
    second_angles = turn_angle(k2_index[:, None] * k2_index[None, :], F2)
    second_cos = jnp.cos(second_angles)
    second_sin = jnp.sin(second_angles)
    inner_twist = turn_angle(k2_index[:, None] * k1_index[None, :], NFFT)
    twist_cos = jnp.cos(inner_twist)
    twist_sin = jnp.sin(inner_twist)
    pieces = lax.all_to_all(section, "tm", split_axis=4, concat_axis=6, tiled=True)
    items = pieces.shape[0]
    points = pieces[:, :, :, :, 0]
    fwd_cos = jnp.einsum("xspikq,qw->xspikw", points, second_cos, precision=highest)
    fwd_sin = jnp.einsum("xspikq,qw->xspikw", points, second_sin, precision=highest)
    real_spec = fwd_cos[:, :, :, 0] + fwd_sin[:, :, :, 1]
    imag_spec = fwd_cos[:, :, :, 1] - fwd_sin[:, :, :, 0]
    real_chirped = real_spec * chirp_cos - imag_spec * chirp_sin
    imag_chirped = real_spec * chirp_sin + imag_spec * chirp_cos
    real_inv = jnp.einsum(
        "xspkw,wn->xspnk", real_chirped, second_cos, precision=highest
    ) - jnp.einsum("xspkw,wn->xspnk", imag_chirped, second_sin, precision=highest)
    imag_inv = jnp.einsum(
        "xspkw,wn->xspnk", real_chirped, second_sin, precision=highest
    ) + jnp.einsum("xspkw,wn->xspnk", imag_chirped, second_cos, precision=highest)
    turned = jnp.stack(
        [real_inv * twist_cos - imag_inv * twist_sin, real_inv * twist_sin + imag_inv * twist_cos],
        axis=3,
    )
    inverted = turned.reshape(items, slots, pols, 2, tm_count, q_cols, k_cols)
    angle_four = turn_angle(
        freq_first[:, None] * jnp.arange(half_rows, dtype=jnp.int32)[None, :], F1
    )
    four_cos = jnp.cos(angle_four)
    four_sin = jnp.sin(angle_four)
    spectra = lax.all_to_all(inverted, "tm", split_axis=4, concat_axis=6, tiled=True)[:, :, :, :, 0]
    last_cos = jnp.einsum("xspiqk,kh->xspiqh", spectra, four_cos, precision=highest)
    last_sin = jnp.einsum("xspiqk,kh->xspiqh", spectra, four_sin, precision=highest)
    real_sig = last_cos[:, :, :, 0] - last_sin[:, :, :, 1]
    imag_sig = last_sin[:, :, :, 0] + last_cos[:, :, :, 1]
    detected = jnp.sum(real_sig * real_sig + imag_sig * imag_sig, axis=2)
    weighted = jnp.sum(detected[:, :, None] * weights[None, :, :, None, None], axis=1)
    partial_power = jnp.swapaxes(weighted, 2, 3)
    moved = lax.all_to_all(partial_power, "tm", split_axis=2, concat_axis=3, tiled=True)
    result = lax.psum_scatter(moved, "grp", scatter_dimension=2, tiled=True)
    return result.reshape(beams, grp_count, -1)


def solution(mesh):
    in_specs = (P(None, None, None, None, ("tm", "grp")), P(None, "tm", None), P(), P())
    out_specs = P(None, None, ("tm", "grp"))
    return jax.shard_map(
        on_device, mesh=mesh, in_specs=in_specs, out_specs=out_specs, check_vma=False
    )
```

profile of v0, /device:TPU:0, one launch (start us, length us, event | category | flops | bytes accessed | tf_op | source)
XLA Modules:
  0.0 514.6 jit_solution(16117838292938271570)
XLA Ops:
  6.7 7.5 %gather_fusion = bf16[24,2,2,8192]{3,2,1,0:T(2,128)(2,1)} fusion(bf16[24,2,2,8192]{3,2,1,0:T(2,128)(2,1)} %bitcast.212, s32[1024]{0:T(1024)S(1)} %pad_clamp_fusion.1), kind=kCustom, calls=%fused_computation | custom fusion | bytes 3145824 | tf_op jit(solution)/shard_map/jit(_take)/gather | solution.py:44
  17.6 5.5 %gather.17 = bf16[1,4,6,2,2,16,8,64]{7,6,5,2,1,4,3,0:T(8,128)(2,1)} reshape(bf16[24,2,2,8192]{3,0,2,1:T(8,128)(2,1)} %copy.57) | data formatting | bytes 3145728 | tf_op jit(solution)/shard_map/jit(_take)/gather | solution.py:44
  27.9 6.9 %reshape.576 = bf16[8,2,49152]{2,1,0:T(2,128)(2,1)} reshape(bf16[8,1,4,6,2,2,16,64]{7,6,5,4,3,2,1,0:T(8,128)(2,1)} %bitcast.207) | data formatting | bytes 3145728
  34.8 44.4 %all_to_all.71 = bf16[8,2,49152]{2,1,0:T(2,128)(2,1)} all-to-all(bf16[8,2,49152]{2,1,0:T(2,128)(2,1)} %reshape.576), channel_id=1, replica_groups=mesh['tm'=8,'grp'=4] {'tm'}, dimensions={0} | all-to-all | bytes 3145728 | tf_op jit(solution)/shard_map/all_to_all | solution.py:49
  79.2 6.8 %reshape.577 = bf16[8,1,4,6,2,2,16,64]{7,6,5,4,3,2,1,0:T(8,128)(2,1)} reshape(bf16[8,2,49152]{2,1,0:T(2,128)(2,1)} %all_to_all.71) | data formatting | bytes 3145728
  95.8 4.8 all-to-all-start.1
  101.3 19.0 %all-to-all-done.1 = bf16[1,4,6,2,2,1,64,128]{7,6,4,3,2,5,0,1:T(8,128)(2,1)} async-done(((bf16[1,4,6,2,2,1,64,128]{7,6,4,3,2,5,0,1:T(8,128)(2,1)}), bf16[1,4,6,2,2,1,64,128]{7,6,4,3,2,5,0,1:T(8,128)(2,1)}, u32[]{:S(2)}, u32[]{:S(2)}) %all-to-all-start.1) | async-done | bytes 1572896 | tf_op jit(solution)/shard_map/all_to_all | solution.py:48
  120.3 8.1 %convolution_bitcast_fusion = f32[1,6,2,2,512,64]{4,5,3,2,1,0:T(8,128)S(1)} fusion(bf16[1,4,6,2,2,1,64,128]{7,6,4,3,2,5,0,1:T(8,128)(2,1)} %all-to-all-done.1, s32[4,128]{1,0:T(4,128)S(1)} %add_add_fusion), kind=kOutput, calls=%fused_computation.9 | convolution fusion | flops 4835508224 | bytes 4720640 | tf_op jit(solution)/shard_map/bgspiqr,grz->bspizq/dot_general | solution.py:65
  128.4 8.3 %convolution_bitcast_fusion.1 = f32[1,6,2,2,512,64]{4,5,3,2,1,0:T(8,128)S(1)} fusion(bf16[1,4,6,2,2,1,64,128]{7,6,4,3,2,5,0,1:T(8,128)(2,1)} %all-to-all-done.1, s32[4,128]{1,0:T(4,128)S(1)} %add_add_fusion), kind=kOutput, calls=%fused_computation.10 | convolution fusion | flops 4835508224 | bytes 4720640 | tf_op jit(solution)/shard_map/bgspiqr,grz->bspizq/dot_general | solution.py:64
  156.3 8.5 %reshape.578 = f32[8,1,98304]{2,1,0:T(1,128)} reshape(f32[8,1,2,6,2,64,64]{6,5,4,3,2,1,0:T(8,128)} %fusion.128) | data formatting | bytes 6291456
  171.8 6.2 %cosine_multiply_fusion = (f32[6,64,512]{2,1,0:T(8,128)}, f32[6,64,512]{2,1,0:T(8,128)}) fusion(s32[6,512]{1,0:T(8,128)S(1)} %fusion.79, s32[6,64]{1,0:T(8,128)S(1)} %broadcast_multiply_fusion, f32[6,64,512]{2,1,0:T(8,128)} %gather_fusion.1, pred[6]{0:T(512)(128)(4,1)S(1)} %compare_and_fusion), kind=kLoop, calls=%fused_computation.91 | loop fusion | flops 3538944 | bytes 2373126 | tf_op jit(solution)/shard_map/div | solution.py:90
  177.9 62.3 %all-to-all-done.2 = f32[8,1,98304]{2,1,0:T(1,128)} async-done(((f32[8,1,98304]{2,1,0:T(1,128)}), f32[8,1,98304]{2,1,0:T(1,128)}, u32[]{:S(2)}, u32[]{:S(2)}) %all-to-all-start.2) | async-done | bytes 3145760 | tf_op jit(solution)/shard_map/all_to_all | solution.py:98
  240.7 10.0 %reduce.3 = f32[8,98304]{1,0:T(8,128)S(1)} reduce(f32[8,1,98304]{2,1,0:T(1,128)} %all-to-all-done.2, f32[]{:T(128)} %broadcast.590), dimensions={1}, to_apply=%all_to_all.56.reduce_sub_computation | reduce | bytes 6291460 | tf_op jit(solution)/shard_map/all_to_all | solution.py:98
  250.7 5.1 reshape.579
  255.9 6.6 %bitcast_bitcast_fusion.1 = f32[1,6,2,2,1,64,8,64]{5,7,2,1,3,6,4,0:T(8,128)} fusion(f32[8,1,2,6,2,64,64]{6,5,4,3,2,1,0:T(8,128)} %reshape.579), kind=kLoop, calls=%fused_computation.190 | loop fusion | bytes 6291456 | tf_op jit(solution)/shard_map/all_to_all | solution.py:98
  262.4 7.0 %copy.64 = f32[1,6,2,2,1,64,8,64]{7,6,5,3,2,1,4,0:T(8,128)} copy(f32[1,6,2,2,1,64,8,64]{5,7,2,1,3,6,4,0:T(8,128)} %bitcast_bitcast_fusion.1) | data formatting | bytes 6291456 | tf_op jit(solution)/shard_map/all_to_all | solution.py:98
  269.4 4.8 reshape.514
  274.2 9.2 %fusion.2 = f32[1,6,2,2,64,512]{5,4,2,1,3,0:T(8,128)S(1)} fusion(f32[6,2,2,64,512]{4,3,2,1,0:T(8,128)S(1)} %reshape.514), kind=kOutput, calls=%fused_computation.11 | convolution fusion | flops 4835508224 | bytes 6291456 | tf_op jit(solution)/shard_map/xspikq,qw->xspikw/dot_general | solution.py:102
  283.4 11.4 %convolution_bitcast_fusion.2 = f32[1,6,2,2,64,512]{5,4,3,2,1,0:T(8,128)S(1)} fusion(f32[6,2,2,64,512]{4,3,2,1,0:T(8,128)S(1)} %reshape.514), kind=kOutput, calls=%fused_computation.12 | convolution fusion | flops 4835508224 | bytes 6291456 | tf_op jit(solution)/shard_map/xspikq,qw->xspikw/dot_general | solution.py:101
  295.9 7.3 %fusion.29 = f32[512,6,2,64]{0,3,2,1:T(8,128)S(1)} fusion(f32[6,2,64,512]{3,2,1,0:T(8,128)S(1)} %get-tuple-element.6), kind=kOutput, calls=%fused_computation.66 | convolution fusion | flops 2419589120 | bytes 3145728 | tf_op jit(solution)/shard_map/xspkw,wn->xspnk/dot_general | solution.py:110
  303.2 7.5 %fusion.27 = f32[512,6,2,64]{0,3,2,1:T(8,128)S(1)} fusion(f32[6,2,64,512]{3,2,1,0:T(8,128)S(1)} %get-tuple-element.6), kind=kOutput, calls=%fused_computation.64 | convolution fusion | flops 2419589120 | bytes 3145728 | tf_op jit(solution)/shard_map/xspkw,wn->xspnk/dot_general | solution.py:107
  310.7 7.3 %convolution_add_fusion = f32[512,6,2,64]{0,3,2,1:T(8,128)S(1)} fusion(f32[512,6,2,64]{0,3,2,1:T(8,128)S(1)} %fusion.29, f32[6,2,64,512]{3,2,1,0:T(8,128)S(1)} %get-tuple-element.5), kind=kOutput, calls=%fused_computation.44 | convolution fusion | flops 2419982336 | bytes 4718592 | tf_op jit(solution)/shard_map/xspkw,wn->xspnk/dot_general | solution.py:112
  318.0 8.1 %fusion.9 = (f32[1,6,2,512,64]{3,4,2,1,0:T(8,128)}, f32[1,6,2,512,64]{3,4,2,1,0:T(8,128)}) fusion(f32[512,6,2,64]{0,3,2,1:T(8,128)S(1)} %convolution_add_fusion, f32[512,64]{0,1:T(8,128)S(1)} %get-tuple-element.14, f32[512,64]{0,1:T(8,128)S(1)} %get-tuple-element.13, f32[512,6,2,64]{0,3,2,1:T(8,128)S(1)} %fusion.27, f32[6,2,64,512]{3,2,1,0:T(8,128)S(1)} %get-tuple-element.5), kind=kOutput, calls=%fused_computation.24 | convolution fusion | flops 2422341632 | bytes 8126464 | tf_op jit(solution)/shard_map/xspkw,wn->xspnk/dot_general | solution.py:109
  338.4 8.5 %reshape.580 = f32[8,1,98304]{2,1,0:T(1,128)} reshape(f32[8,1,2,6,2,64,64]{6,5,4,3,2,1,0:T(8,128)} %fusion.127) | data formatting | bytes 6291456
  352.0 69.6 %all-to-all-done.3 = f32[8,1,98304]{2,1,0:T(1,128)S(1)} async-done(((f32[8,1,98304]{2,1,0:T(1,128)}), f32[8,1,98304]{2,1,0:T(1,128)S(1)}, u32[]{:S(2)}, u32[]{:S(2)}) %all-to-all-start.3) | async-done | bytes 3145760 | tf_op jit(solution)/shard_map/all_to_all | solution.py:123
  421.6 11.2 %reduce.4 = f32[8,98304]{1,0:T(8,128)} reduce(f32[8,1,98304]{2,1,0:T(1,128)S(1)} %all-to-all-done.3, f32[]{:T(128)} %broadcast.590), dimensions={1}, to_apply=%all_to_all.59.reduce_sub_computation | reduce | bytes 6291460 | tf_op jit(solution)/shard_map/all_to_all | solution.py:123
  432.7 7.0 %reshape.581 = f32[8,1,2,6,2,64,64]{6,5,4,3,2,1,0:T(8,128)} reshape(f32[8,98304]{1,0:T(8,128)} %reduce.4) | data formatting | bytes 6291456
  439.7 6.7 %bitcast_bitcast_fusion = f32[1,6,2,2,1,64,8,64]{5,7,2,1,3,6,4,0:T(8,128)} fusion(f32[8,1,2,6,2,64,64]{6,5,4,3,2,1,0:T(8,128)} %reshape.581), kind=kLoop, calls=%fused_computation.189 | loop fusion | bytes 6291456 | tf_op jit(solution)/shard_map/all_to_all | solution.py:123
  446.4 6.5 %copy.70 = f32[1,6,2,2,1,64,8,64]{7,6,5,3,2,1,4,0:T(8,128)} copy(f32[1,6,2,2,1,64,8,64]{5,7,2,1,3,6,4,0:T(8,128)} %bitcast_bitcast_fusion) | data formatting | bytes 6291456 | tf_op jit(solution)/shard_map/all_to_all | solution.py:123
  453.0 4.8 reshape.515
  468.5 12.5 %all_to_all.72 = f32[8,1,8192]{2,1,0:T(1,128)S(1)} all-to-all(f32[8,1,8192]{2,1,0:T(1,128)S(1)} %reshape.582), channel_id=1, replica_groups=mesh['tm'=8,'grp'=4] {'tm'}, dimensions={0} | all-to-all | bytes 524288 | tf_op jit(solution)/shard_map/all_to_all | solution.py:131
  487.7 18.3 %reduce-scatter.2.cloned.1.call-done = f32[1,4,8,512]{3,2,1,0:T(8,128)} async-done(((f32[1,4,32,512]{3,2,1,0:T(8,128)}), f32[1,4,8,512]{3,2,1,0:T(8,128)}) %reduce-scatter.2.cloned.1.call-update) | async-done | bytes 65552 | tf_op jit(solution)/shard_map/reduce_scatter | solution.py:132
  (73 shorter events, 82.9 us)
Async XLA Ops:
  6.5 163.6 %copy-start = (f32[24,64,512]{2,1,0:T(8,128)S(1)}, f32[24,64,512]{2,1,0:T(8,128)}, u32[]{:S(2)}) copy-start(f32[24,64,512]{2,1,0:T(8,128)} %param.5) | copy-start | bytes 9437188
  95.8 24.5 %all-to-all-start.1 = ((bf16[1,4,6,2,2,1,64,128]{7,6,4,3,2,5,0,1:T(8,128)(2,1)}), bf16[1,4,6,2,2,1,64,128]{7,6,4,3,2,5,0,1:T(8,128)(2,1)}, u32[]{:S(2)}, u32[]{:S(2)}) async-start(bf16[1,4,6,2,2,1,64,128]{7,6,4,3,2,5,0,1:T(8,128)(2,1)} %copy.60), calls=%async_computation.1 | async-start | bytes 3145728 | tf_op jit(solution)/shard_map/all_to_all | solution.py:48
  150.1 2.8 copy-start.3
  164.8 4.6 copy-start.2
  164.8 75.4 %all-to-all-start.2 = ((f32[8,1,98304]{2,1,0:T(1,128)}), f32[8,1,98304]{2,1,0:T(1,128)}, u32[]{:S(2)}, u32[]{:S(2)}) async-start(f32[8,1,98304]{2,1,0:T(1,128)} %reshape.578), calls=%async_computation.2 | async-start | bytes 6291456 | tf_op jit(solution)/shard_map/all_to_all | solution.py:98
  283.4 11.4 %copy-start.5 = (f32[6,64,512]{2,1,0:T(8,128)S(1)}, f32[6,64,512]{2,1,0:T(8,128)}, u32[]{:S(2)}) copy-start(f32[6,64,512]{2,1,0:T(8,128)} %get-tuple-element.11) | copy-start | bytes 2359300
  283.4 11.4 %copy-start.6 = (f32[6,64,512]{2,1,0:T(8,128)S(1)}, f32[6,64,512]{2,1,0:T(8,128)}, u32[]{:S(2)}) copy-start(f32[6,64,512]{2,1,0:T(8,128)} %get-tuple-element.12) | copy-start | bytes 2359300
  333.2 1.9 copy-start.4
  346.9 4.3 copy-start.7
  346.9 74.6 %all-to-all-start.3 = ((f32[8,1,98304]{2,1,0:T(1,128)}), f32[8,1,98304]{2,1,0:T(1,128)S(1)}, u32[]{:S(2)}, u32[]{:S(2)}) async-start(f32[8,1,98304]{2,1,0:T(1,128)} %reshape.580), calls=%async_computation.3 | async-start | bytes 6291456 | tf_op jit(solution)/shard_map/all_to_all | solution.py:123
  350.7 155.3 %reduce-scatter.2.cloned.1.call-start = ((), (), s32[]{:S(2)}) async-start(), calls=%async_computation.6 | async-start | bytes 327680 | tf_op jit(solution)/shard_map/reduce_scatter | solution.py:132
  483.5 24.1 %copy-start.1 = (f32[24,64,512]{2,1,0:T(8,128)S(1)}, f32[24,64,512]{2,1,0:T(8,128)}, u32[]{:S(2)}) copy-start(f32[24,64,512]{2,1,0:T(8,128)} %param.5) | copy-start | bytes 9437188
Sparse Core Ops, SparseCore 0:
  487.8 18.1 reduce-scatter.1
where the time goes:
time: 522 us; the launch traced here: 515 us
  waiting for transfers between devices  169 us (32%)
  local copies, waits for them, and re-layouts  142 us (27%)
  matrix products  76.7 us (15%)
  blocking collectives  56.9 us (11%)
  other arithmetic  42.6 us (8%)
  between operations  13.9 us (3%)
  starting transfers between devices  13.7 us (3%)
    all_to_all x1, waiting for transfers between devices, on_device(): lax.all_to_all(inverted, 'tm', split_axis=4, concat_axis=6, tiled=True)  69.6 us
    all_to_all x1, waiting for transfers between devices, on_device(): lax.all_to_all(section, 'tm', split_axis=4, concat_axis=6, tiled=True)  62.3 us
    unnamed x24, local copies, waits for them, and re-layouts  46 us
    all_to_all x1, blocking collectives, on_device(): lax.all_to_all(outgoing, 'tm', split_axis=5, concat_axis=7, tiled=True)  44.4 us
    all_to_all x1, waiting for transfers between devices, on_device(): lax.all_to_all(lax.all_to_all(outgoing, 'tm', split_axis=5, concat_axis=7...  19 us
    reduce_scatter x1, waiting for transfers between devices, on_device(): result = lax.psum_scatter(moved, 'grp', scatter_dimension=2, tiled=True)  18.3 us
    gather x3, local copies, waits for them, and re-layouts, on_device(): jnp.take(voltages, slot_table, axis=1)  16.5 us
    all_to_all x3, local copies, waits for them, and re-layouts, on_device(): lax.all_to_all(section, 'tm', split_axis=4, concat_axis=6, tiled=True)  14.1 us
  transfers between devices with their start and end apart: 4, of which 4 were waited for; matrix products, arithmetic and copies ran while one was open for 2% of the time, Pallas kernels for 0%

commit v1 on v0

v1 whole, which is shorter than its diff:
```python
import functools
import math

import jax
import jax.numpy as jnp
import numpy as np
from jax import lax
from jax.experimental import pallas as pl
from jax.experimental.pallas import tpu as pltpu
from jax.sharding import PartitionSpec as P

f32 = jnp.float32
bf16 = jnp.bfloat16


def split(values):
    high = values.astype(bf16)
    return high, (values - high.astype(f32)).astype(bf16)


def np_split(values):
    high = values.astype(np.float32).astype(bf16)
    low = (values - high.astype(np.float64)).astype(np.float32).astype(bf16)
    return np.asarray(high), np.asarray(low)


@functools.lru_cache(None)
def tables(f):
    index = np.arange(f)
    product = index[:, None] * index[None, :]
    angle = 2.0 * np.pi * (product % f) / f
    c, s = np.cos(angle), np.sin(angle)
    forward = np.block([[c, -s], [s, c]])
    inverse = np.block([[c, s], [-s, c]])
    twist = 2.0 * np.pi * product / (f * f)
    return (
        *np_split(forward),
        *np_split(inverse),
        np.cos(twist).astype(np.float32),
        np.sin(twist).astype(np.float32),
    )


@functools.lru_cache(None)
def turn_polynomials():
    nodes = 0.125 + 0.13 * np.cos(np.pi * (np.arange(200) + 0.5) / 200)
    root = np.sqrt(np.abs(nodes))
    fits = []
    for values, degree in (
        (np.cos(2 * np.pi * root), 8),
        (np.sin(2 * np.pi * root) / root, 8),
    ):
        keep = nodes > 0
        fit = np.polynomial.Chebyshev.fit(nodes[keep], values[keep], degree, domain=[0, 0.25])
        fits.append([float(x) for x in fit.convert(kind=np.polynomial.Polynomial).coef])
    return fits


def horner(q, coefficients):
    total = jnp.full_like(q, coefficients[-1])
    for x in coefficients[-2::-1]:
        total = total * q + x
    return total


def chirp_tables(shift, phase, k1):
    f = phase.shape[1]
    nfft = f * f
    rows = k1 + lax.broadcasted_iota(jnp.int32, phase.shape, 0)
    cols = lax.broadcasted_iota(jnp.int32, phase.shape, 1)
    ramp = (rows * shift + f * ((cols * shift) & (f - 1))) & (nfft - 1)
    turns = phase * (0.5 / math.pi) + ramp.astype(f32) * (1.0 / nfft)
    rest = turns - jnp.round(turns)
    q = rest * rest
    cos_fit, sin_fit = turn_polynomials()
    scale = 1.0 / nfft
    return horner(q, cos_fit) * scale, horner(q, sin_fit) * (rest * scale)


def mm(a, b):
    return jnp.dot(a, b, preferred_element_type=f32)


def three(values, high, low):
    rows = values.shape[0]
    vh, vl = split(values)
    both = mm(jnp.concatenate([vh, vl], axis=0), high)
    return both[:rows] + both[rows:] + mm(vh, low)


def rows_step(i, z, g2h, g2l, g3h, g3l, tc, ts, cc, cs, vh, vl, tile):
    f = tc.shape[0]
    top = pl.ds(pl.multiple_of(i * tile, tile), tile)
    bot = pl.ds(pl.multiple_of(f + i * tile, tile), tile)
    lhs = jnp.concatenate([g3h[top], g3h[bot], g3l[top], g3l[bot]], axis=0)
    r = mm(lhs, z)
    yr = r[:tile] + r[2 * tile : 3 * tile]
    yi = r[tile : 2 * tile] + r[3 * tile :]
    c, s = tc[top], ts[top]
    spec = three(jnp.concatenate([yr * c + yi * s, yi * c - yr * s], axis=1), g2h[...], g2l[...])
    zr, zi = spec[:, :f], spec[:, f:]
    hc, hs = cc[top], cs[top]
    v = three(jnp.concatenate([zr * hc - zi * hs, zr * hs + zi * hc], axis=1), g3h[...], g3l[...])
    vr, vi = v[:, :f], v[:, f:]
    ah, al = split(vr * c - vi * s)
    vh[top], vl[top] = ah, al
    ah, al = split(vr * s + vi * c)
    vh[bot], vl[bot] = ah, al


def last_step(g2h, g2l, vh, vl):
    f = vh.shape[1]
    half = f // 2
    highs = [g2h[:half], g2h[f : f + half]]
    lhs = jnp.concatenate(highs + [g2l[:half], g2l[f : f + half]], axis=0)
    r = mm(lhs, vh[...])
    sig = r[:f] + r[f:] + mm(jnp.concatenate(highs, axis=0), vl[...])
    sr, si = sig[:half], sig[half:]
    return sr * sr + si * si


def local_kernel(shift, z, phase, g2h, g2l, g3h, g3l, tc, ts, power, cc, cs, vh, vl, *, tile):
    f = phase.shape[0]
    pols = z.shape[0]

    def chirp_step(i, carry):
        rows = pl.ds(pl.multiple_of(i * 64, 64), 64)
        cc[rows], cs[rows] = chirp_tables(shift[0], phase[rows], i * 64)
        return carry

    lax.fori_loop(0, f // 64, chirp_step, 0)
    power[...] = jnp.zeros_like(power)

    def pol_step(p, carry):
        def step(i, inner):
            rows_step(i, z[p], g2h, g2l, g3h, g3l, tc, ts, cc, cs, vh, vl, tile)
            return inner

        lax.fori_loop(0, f // tile, step, 0)
        power[...] += last_step(g2h, g2l, vh, vl)
        return carry

    lax.fori_loop(0, pols, pol_step, 0)


def channel_power(shift, z, phase):
    f = phase.shape[0]
    tile = f // 2
    smem = pl.BlockSpec(memory_space=pltpu.SMEM)
    vmem = pl.BlockSpec(memory_space=pltpu.VMEM)
    return pl.pallas_call(
        functools.partial(local_kernel, tile=tile),
        out_shape=jax.ShapeDtypeStruct((f // 2, f), f32),
        in_specs=[smem] + [vmem] * 8,
        out_specs=vmem,
        scratch_shapes=[
            pltpu.VMEM((f, f), f32),
            pltpu.VMEM((f, f), f32),
            pltpu.VMEM((2 * f, f), bf16),
            pltpu.VMEM((2 * f, f), bf16),
        ],
        compiler_params=pltpu.CompilerParams(vmem_limit_bytes=56 * 1024 * 1024),
    )(shift, z, phase, *(jnp.asarray(t) for t in tables(f)))


def on_device(voltages, chirp_phase, intersection, group_of):
    tm_count = lax.axis_size("tm")
    grp_count = lax.axis_size("grp")
    devices = tm_count * grp_count
    tm_rank = lax.axis_index("tm")
    grp_rank = lax.axis_index("grp")
    me = tm_rank * grp_count + grp_rank
    beams, chans, pols, _, local_len = voltages.shape
    f = chirp_phase.shape[2]
    rows = local_len // f
    groups = 4
    owners = np.arange(chans) * devices // chans
    owned = np.zeros(devices, np.int32)
    owned[owners] = np.arange(chans)
    active = np.zeros(devices, np.float32)
    active[owners] = 1.0
    mine = jnp.asarray(owned)[me]
    out = jnp.take(voltages[0], owned, axis=0)
    got = lax.all_to_all(out, ("tm", "grp"), split_axis=0, concat_axis=0, tiled=True)
    z = jnp.transpose(got.reshape(devices, pols, 2, rows, f), (1, 2, 0, 3, 4)).reshape(pols, 2 * f, f)
    column = jnp.asarray(owned.reshape(tm_count, grp_count))[:, grp_rank]
    phase = lax.all_to_all(
        jnp.take(chirp_phase, column, axis=0), "tm", split_axis=0, concat_axis=0, tiled=True
    ).reshape(f, f)
    power = channel_power(intersection[mine][None], z, phase)
    moved = lax.all_to_all(
        power.reshape(devices, -1), ("tm", "grp"), split_axis=0, concat_axis=0, tiled=True
    )
    member = (group_of[None, :] == jnp.arange(groups, dtype=jnp.int32)[:, None]).astype(f32)
    counts = jnp.sum(member, axis=1, keepdims=True)
    weights = jnp.take(member, owned, axis=1) * active[None, :] / (2.0 * counts)
    result = jnp.sum(weights[:, :, None] * moved[None], axis=1)
    return result[None]


def solution(mesh):
    in_specs = (P(None, None, None, None, ("tm", "grp")), P(None, "tm", None), P(), P())
    out_specs = P(None, None, ("tm", "grp"))
    return jax.shard_map(
        on_device, mesh=mesh, in_specs=in_specs, out_specs=out_specs, check_vma=False
    )
```

time: 522 us -> 151 us (0.29); the launches traced: 515 us -> 151 us
  local copies, waits for them, and re-layouts: 142 us -> 22.6 us
  waiting for transfers between devices: 169 us -> 74.4 us
  matrix products: 76.7 us -> 0 us
  blocking collectives: 56.9 us -> 0 us
  other arithmetic: 42.6 us -> 4.47 us
  Pallas kernels: 0 us -> 31.6 us
  between operations: 13.9 us -> 2.07 us
    dot_general x10 -> x0, matrix products: 76.7 us -> none  [the longest x1 11.4 us: on_device(): jnp.einsum('xspikq,qw->xspikw', points, second_cos, precision=highest)]
    all_to_all x3, waiting for transfers between devices: 151 us -> 74.4 us  [the longest x1 44.7 us: on_device(): lax.all_to_all(out, ('tm', 'grp'), split_axis=0, concat_axis=0, tiled=True)]
    all_to_all x2 -> x0, blocking collectives: 56.9 us -> none  [the longest x1 44.4 us: on_device(): lax.all_to_all(outgoing, 'tm', split_axis=5, concat_axis=7, tiled=True)]
    unnamed x24 -> x13, local copies, waits for them, and re-layouts: 46 us -> 1.38 us
    all_to_all x11 -> x1, local copies, waits for them, and re-layouts: 41.4 us -> 2.48 us  [on_device(): lax.all_to_all(power.reshape(devices, -1), ('tm', 'grp'), split_axis=0, c...]
    pallas_call x0 -> x1, Pallas kernels: none -> 31.6 us  [channel_power(): pl.pallas_call(functools.partial(local_kernel, tile=tile), out_shape=jax....]
    another operation x10 -> x0, local copies, waits for them, and re-layouts: 30.7 us -> none  [the longest x4 13.5 us: on_device(): jnp.stack([real_first * twist_one_cos + imag_first * twist_one_sin, imag_...]
    all_to_all x3 -> x0, other arithmetic: 22.4 us -> none  [the longest x1 11.2 us: on_device(): lax.all_to_all(inverted, 'tm', split_axis=4, concat_axis=6, tiled=True)]
  transfers between devices with their start and end apart: 4 -> 3, of which waited for: 4 -> 3; matrix products, arithmetic and copies ran while one was open for 2% -> 9% of each run, Pallas kernels for 0% -> 0%
where the time goes in v1:
time: 151 us
  waiting for transfers between devices  74.4 us (49%)
  Pallas kernels  31.6 us (21%)
  local copies, waits for them, and re-layouts  22.6 us (15%)
  starting transfers between devices  15.4 us (10%)
  other arithmetic  4.47 us (3%)
  between operations  2.07 us (1%)
    all_to_all x1, waiting for transfers between devices, on_device(): lax.all_to_all(out, ('tm', 'grp'), split_axis=0, concat_axis=0, tiled=True)  44.7 us
    pallas_call x1, Pallas kernels, channel_power(): pl.pallas_call(functools.partial(local_kernel, tile=tile), out_shape=jax....  31.6 us
    all_to_all x1, waiting for transfers between devices, on_device(): lax.all_to_all(jnp.take(chirp_phase, column, axis=0), 'tm', split_axis=0,...  15.1 us
    all_to_all x1, waiting for transfers between devices, on_device(): lax.all_to_all(power.reshape(devices, -1), ('tm', 'grp'), split_axis=0, c...  14.6 us
    gather x1, local copies, waits for them, and re-layouts, on_device(): out = jnp.take(voltages[0], owned, axis=0)  7.7 us
    reshape x2, local copies, waits for them, and re-layouts, on_device(): got.reshape(devices, pols, 2, rows, f)  7.61 us
    all_to_all x1, starting transfers between devices, on_device(): lax.all_to_all(out, ('tm', 'grp'), split_axis=0, concat_axis=0, tiled=True)  7.43 us
    all_to_all x1, starting transfers between devices, on_device(): lax.all_to_all(jnp.take(chirp_phase, column, axis=0), 'tm', split_axis=0,...  4.24 us
  transfers between devices with their start and end apart: 3, of which 3 were waited for; matrix products, arithmetic and copies ran while one was open for 9% of the time, Pallas kernels for 0%

profile of v1, /device:TPU:0, one launch (start us, length us, event | category | flops | bytes accessed | tf_op | source)
XLA Modules:
  0.0 150.6 jit_solution(14795597389890143167)
XLA Ops:
  0.0 0.0 copy-start
  0.0 0.8 pad_clamp_fusion.1
  0.8 7.7 %gather_fusion.1 = bf16[32,2,2,8192]{3,2,1,0:T(2,128)(2,1)} fusion(bf16[24,2,2,8192]{3,2,1,0:T(2,128)(2,1)} %bitcast.17, s32[1024]{0:T(1024)S(1)} %pad_clamp_fusion.1), kind=kCustom, calls=%fused_computation.1 | custom fusion | bytes 4194432 | tf_op jit(solution)/shard_map/jit(_take)/gather | solution.py:183
  8.5 7.4 %all-to-all-start = ((bf16[32,2,2,8192]{3,2,1,0:T(2,128)(2,1)}), bf16[32,2,2,8192]{3,2,1,0:T(2,128)(2,1)}, u32[]{:S(2)}, u32[]{:S(2)}) async-start(bf16[32,2,2,8192]{3,2,1,0:T(2,128)(2,1)} %gather_fusion.1), calls=%async_computation | async-start | bytes 4194304 | tf_op jit(solution)/shard_map/all_to_all | solution.py:184
  16.0 0.0 copy-done.5
  16.0 0.0 copy-done
  16.0 1.6 %gather_fusion.2 = f32[8,64,512]{2,1,0:T(8,128)} fusion(f32[24,64,512]{2,1,0:T(8,128)S(1)} %copy-done, s32[1024]{0:T(1024)S(1)} %pad_clamp_fusion), kind=kCustom, calls=%fused_computation.2 | custom fusion | bytes 2097184 | tf_op jit(solution)/shard_map/jit(_take)/gather | solution.py:188
  17.6 0.0 copy-start.3
  17.6 0.0 copy-start.4
  17.7 2.4 %broadcast_select_fusion = f32[8,64,512]{2,1,0:T(8,128)} fusion(f32[8,64,512]{2,1,0:T(8,128)} %gather_fusion.2, pred[8]{0:T(512)(128)(4,1)S(1)} %and_bitcast_fusion), kind=kLoop, calls=%fused_computation.5 | loop fusion | flops 262144 | bytes 2097160 | tf_op jit(solution)/shard_map/jit(_take)/select_n | solution.py:188
  20.1 44.7 %all-to-all-done = bf16[32,2,2,8192]{3,2,1,0:T(2,128)(2,1)} async-done(((bf16[32,2,2,8192]{3,2,1,0:T(2,128)(2,1)}), bf16[32,2,2,8192]{3,2,1,0:T(2,128)(2,1)}, u32[]{:S(2)}, u32[]{:S(2)}) %all-to-all-start) | async-done | bytes 2097184 | tf_op jit(solution)/shard_map/all_to_all | solution.py:184
  64.8 4.2 %all-to-all-start.1 = ((f32[8,64,512]{2,1,0:T(8,128)}), f32[8,64,512]{2,1,0:T(8,128)}, u32[]{:S(2)}, u32[]{:S(2)}) async-start(f32[8,64,512]{2,1,0:T(8,128)} %broadcast_select_fusion), calls=%async_computation.1 | async-start | bytes 2097152 | tf_op jit(solution)/shard_map/all_to_all | solution.py:187
  69.1 0.0 copy-done.3
  69.1 0.6 dynamic_slice.9
  71.6 0.0 copy-done.4
  71.6 0.6 dynamic_slice.10.shift
  72.2 4.4 %reshape.71 = bf16[32,2,2,16,512]{4,3,2,1,0:T(8,128)(2,1)} reshape(bf16[32,2,2,8192]{3,2,1,0:T(2,128)(2,1)} %all-to-all-done) | data formatting | bytes 4194304 | tf_op jit(solution)/shard_map/reshape | solution.py:185
  76.6 3.2 %copy.20 = bf16[32,2,2,16,512]{4,3,0,2,1:T(8,128)(2,1)} copy(bf16[32,2,2,16,512]{4,3,2,1,0:T(8,128)(2,1)} %reshape.71) | data formatting | bytes 4194304 | tf_op jit(solution)/shard_map/reshape | solution.py:185
  79.8 15.1 %all-to-all-done.1 = f32[8,64,512]{2,1,0:T(8,128)} async-done(((f32[8,64,512]{2,1,0:T(8,128)}), f32[8,64,512]{2,1,0:T(8,128)}, u32[]{:S(2)}, u32[]{:S(2)}) %all-to-all-start.1) | async-done | bytes 1048608 | tf_op jit(solution)/shard_map/all_to_all | solution.py:187
  94.9 31.6 %shard_map.127 = f32[256,512]{1,0:T(8,128)} custom-call(s32[1]{0:T(128)} %dynamic_slice.10.shift, bf16[2,1024,512]{2,1,0:T(8,128)(2,1)} %bitcast.16, f32[512,512]{1,0:T(8,128)} %bitcast.7.phase, bf16[1024,1024]{1,0:T(8,128)(2,1)} %constant.80.clone.g2h, bf16[1024,1024]{1,0:T(8,128)(2,1)} %constant.81.clone.g2l, bf16[1024,1024]{1,0:T(8,128)(2,1)} %constant.82.clone.g3h, ...), custom_call_target="tpu_custom_call" | custom-call | tf_op jit(solution)/shard_map/pallas_call | solution.py:151
  126.5 2.5 %all_to_all.16 = f32[32,1,4096]{2,1,0:T(1,128)} reshape(f32[256,512]{1,0:T(8,128)} %shard_map.127) | data formatting | bytes 1048576 | tf_op jit(solution)/shard_map/all_to_all | solution.py:191
  129.0 3.8 %all-to-all-start.2 = ((f32[32,1,4096]{2,1,0:T(1,128)}), f32[32,1,4096]{2,1,0:T(1,128)}, u32[]{:S(2)}, u32[]{:S(2)}) async-start(f32[32,1,4096]{2,1,0:T(1,128)} %all_to_all.16), calls=%async_computation.2 | async-start | bytes 1048576 | tf_op jit(solution)/shard_map/all_to_all | solution.py:191
  132.8 0.0 copy-done.2
  132.8 0.1 fusion
  132.9 0.6 gather_fusion
  133.4 0.1 fusion.1
  133.5 0.0 copy-done.1
  133.5 0.1 divide_bitcast_fusion
  133.6 0.1 copy.19
  133.7 14.6 %all-to-all-done.2 = f32[32,1,4096]{2,1,0:T(1,128)} async-done(((f32[32,1,4096]{2,1,0:T(1,128)}), f32[32,1,4096]{2,1,0:T(1,128)}, u32[]{:S(2)}, u32[]{:S(2)}) %all-to-all-start.2) | async-done | bytes 524320 | tf_op jit(solution)/shard_map/all_to_all | solution.py:191
  148.3 1.3 copy.24
  149.7 1.0 multiply_reduce_fusion
  (7 shorter events, 0.0 us)
Async XLA Ops:
  0.0 16.0 %copy-start = (f32[24,64,512]{2,1,0:T(8,128)S(1)}, f32[24,64,512]{2,1,0:T(8,128)}, u32[]{:S(2)}) copy-start(f32[24,64,512]{2,1,0:T(8,128)} %param.14) | copy-start | bytes 9437188
  8.5 7.4 %copy-start.5 = (s32[8,4]{0,1:T(4,128)S(1)}, s32[8,4]{0,1:T(4,128)}, u32[]{:S(2)}) copy-start(s32[8,4]{0,1:T(4,128)} %constant.79.clone) | copy-start | bytes 388
  8.5 56.3 %all-to-all-start = ((bf16[32,2,2,8192]{3,2,1,0:T(2,128)(2,1)}), bf16[32,2,2,8192]{3,2,1,0:T(2,128)(2,1)}, u32[]{:S(2)}, u32[]{:S(2)}) async-start(bf16[32,2,2,8192]{3,2,1,0:T(2,128)(2,1)} %gather_fusion.1), calls=%async_computation | async-start | bytes 4194304 | tf_op jit(solution)/shard_map/all_to_all | solution.py:184
  17.6 51.4 %copy-start.3 = (s32[32]{0:T(128)S(1)}, s32[32]{0:T(128)}, u32[]{:S(2)}) copy-start(s32[32]{0:T(128)} %constant.78.clone) | copy-start | bytes 388
  17.6 54.0 %copy-start.4 = (s32[24]{0:T(128)S(1)}, s32[24]{0:T(128)}, u32[]{:S(2)}) copy-start(s32[24]{0:T(128)} %param.15) | copy-start | bytes 292
  64.8 30.1 %all-to-all-start.1 = ((f32[8,64,512]{2,1,0:T(8,128)}), f32[8,64,512]{2,1,0:T(8,128)}, u32[]{:S(2)}, u32[]{:S(2)}) async-start(f32[8,64,512]{2,1,0:T(8,128)} %broadcast_select_fusion), calls=%async_computation.1 | async-start | bytes 2097152 | tf_op jit(solution)/shard_map/all_to_all | solution.py:187
  126.5 6.3 %copy-start.2 = (s32[24]{0:T(128)S(1)}, s32[24]{0:T(128)}, u32[]{:S(2)}) copy-start(s32[24]{0:T(128)} %param.16) | copy-start | bytes 292
  126.5 7.0 %copy-start.1 = (f32[32]{0:T(128)S(1)}, f32[32]{0:T(128)}, u32[]{:S(2)}) copy-start(f32[32]{0:T(128)} %constant.94) | copy-start | bytes 388
  129.0 19.3 %all-to-all-start.2 = ((f32[32,1,4096]{2,1,0:T(1,128)}), f32[32,1,4096]{2,1,0:T(1,128)}, u32[]{:S(2)}, u32[]{:S(2)}) async-start(f32[32,1,4096]{2,1,0:T(1,128)} %all_to_all.16), calls=%async_computation.2 | async-start | bytes 1048576 | tf_op jit(solution)/shard_map/all_to_all | solution.py:191

commit v2 on v1

--- a/solution.py
+++ b/solution.py
@@ -163,6 +163,216 @@
     )(shift, z, phase, *(jnp.asarray(t) for t in tables(f)))
 
 
+MESH = pl.DeviceIdType.MESH
+
+
+def staggered(chans, tm_count, grp_count):
+    return grp_count == 4 and chans == tm_count * (grp_count - 1)
+
+
+def owner_of(c):
+    t, k = lax.div(c, 3), lax.rem(c, 3)
+    a = lax.rem(lax.div(t, 2) + lax.rem(t, 2), 2)
+    return t, k + a * lax.div(k + 1, 2)
+
+
+def channel_at(t, j):
+    a = lax.rem(lax.div(t, 2) + lax.rem(t, 2), 2)
+    return 3 * t + j - a * lax.div(j + 3, 4), j != 3 - 2 * a
+
+
+def fused_kernel(
+    shift, weights, volt, chirp, h_g2h, h_g2l, h_g3h, h_g3l, h_tc, h_ts, out,
+    z, phase, gathered, power, g2h, g2l, g3h, g3l, tc, ts, cc, cs, vh, vl,
+    table_sem, volt_send, volt_recv, chirp_send, chirp_recv, power_send, power_recv,
+    *, tm_count, grp_count, tile,
+):
+    t, j = lax.axis_index("tm"), lax.axis_index("grp")
+    devices = tm_count * grp_count
+    me = t * grp_count + j
+    chans, pols, _, rows, f = volt.shape
+    k_rows = chirp.shape[1]
+    t_rows = gathered.shape[1]
+    mine, active = channel_at(t, j)
+
+    pairs = [(h_g2h, g2h), (h_g2l, g2l), (h_g3h, g3h), (h_g3l, g3l), (h_tc, tc), (h_ts, ts)]
+    loads = [pltpu.make_async_copy(a, b, table_sem.at[i]) for i, (a, b) in enumerate(pairs)]
+    for load in loads:
+        load.start()
+
+    barrier = pltpu.get_barrier_semaphore()
+
+    def greet(i, carry):
+        d = lax.rem(me + i, devices)
+        pl.semaphore_signal(
+            barrier, inc=1, device_id=(lax.div(d, grp_count), lax.rem(d, grp_count)), device_id_type=MESH
+        )
+        return carry
+
+    lax.fori_loop(1, devices, greet, 0)
+    pl.semaphore_wait(barrier, devices - 1)
+
+    k_slot = pl.ds(pl.multiple_of(t * k_rows, k_rows), k_rows)
+    z_slot = pl.ds(pl.multiple_of(me * rows, rows), rows)
+    first = 3 * t
+
+    def chirp_copy(c, ot, oj):
+        return pltpu.make_async_remote_copy(
+            src_ref=chirp.at[c], dst_ref=phase.at[k_slot], send_sem=chirp_send.at[c],
+            recv_sem=chirp_recv, device_id=(ot, oj), device_id_type=MESH,
+        )
+
+    def volt_copy(c, p, ot, oj):
+        return pltpu.make_async_remote_copy(
+            src_ref=volt.at[c, p], dst_ref=z.at[p, :, z_slot], send_sem=volt_send.at[p, c],
+            recv_sem=volt_recv.at[p], device_id=(ot, oj), device_id_type=MESH,
+        )
+
+    def over_channels(start, act):
+        def step(i, carry):
+            c = lax.rem(start + i, chans)
+            ot, oj = owner_of(c)
+            act(c, ot, oj)
+            return carry
+
+        lax.fori_loop(0, chans, step, 0)
+
+    def send_chirp(c, ot, oj):
+        @pl.when((oj == j) & (ot != t))
+        def _():
+            chirp_copy(c, ot, oj).start()
+
+    over_channels(first, send_chirp)
+
+    @pl.when(active)
+    def _():
+        pltpu.make_async_copy(chirp.at[mine], phase.at[k_slot], chirp_recv).start()
+
+    def send_pol(p, carry):
+        def send_volt(c, ot, oj):
+            @pl.when((oj != j) | (ot != t))
+            def _():
+                volt_copy(c, p, ot, oj).start()
+
+        over_channels(first, send_volt)
+
+        @pl.when(active)
+        def _():
+            pltpu.make_async_copy(volt.at[mine, p], z.at[p, :, z_slot], volt_recv.at[p]).start()
+
+        return carry
+
+    lax.fori_loop(0, pols, send_pol, 0)
+    for load in loads:
+        load.wait()
+
+    def power_copy(d):
+        return pltpu.make_async_remote_copy(
+            src_ref=power.at[pl.ds(pl.multiple_of(d * t_rows, t_rows), t_rows)],
+            dst_ref=gathered.at[mine], send_sem=power_send.at[d], recv_sem=power_recv,
+            device_id=(lax.div(d, grp_count), lax.rem(d, grp_count)), device_id_type=MESH,
+        )
+
+    @pl.when(active)
+    def _():
+        pltpu.make_async_copy(phase, phase, chirp_recv).wait()
+
+        def chirp_step(i, carry):
+            part = pl.ds(pl.multiple_of(i * 64, 64), 64)
+            cc[part], cs[part] = chirp_tables(shift[0], phase[part], i * 64)
+            return carry
+
+        lax.fori_loop(0, f // 64, chirp_step, 0)
+        power[...] = jnp.zeros_like(power)
+
+        def pol_step(p, carry):
+            pltpu.make_async_copy(z.at[p], z.at[p], volt_recv.at[p]).wait()
+
+            def step(i, inner):
+                samples = z[p].reshape(2 * f, f)
+                rows_step(i, samples, g2h, g2l, g3h, g3l, tc, ts, cc, cs, vh, vl, tile)
+                return inner
+
+            lax.fori_loop(0, f // tile, step, 0)
+            power[...] += last_step(g2h, g2l, vh, vl)
+            return carry
+
+        lax.fori_loop(0, pols, pol_step, 0)
+
+        def send_power(i, carry):
+            power_copy(lax.rem(me + i, devices)).start()
+            return carry
+
+        lax.fori_loop(1, devices, send_power, 0)
+        own = power.at[pl.ds(pl.multiple_of(me * t_rows, t_rows), t_rows)]
+        pltpu.make_async_copy(own, gathered.at[mine], power_recv).start()
+
+    pltpu.make_async_copy(gathered, gathered, power_recv).wait()
+    for g in range(out.shape[0]):
+        total = weights[g * chans] * gathered[0]
+        for c in range(1, chans):
+            total = total + weights[g * chans + c] * gathered[c]
+        out[g] = total
+
+    def wait_chirp(c, ot, oj):
+        @pl.when((oj == j) & (ot != t))
+        def _():
+            chirp_copy(c, ot, oj).wait_send()
+
+    def wait_volt(c, ot, oj):
+        @pl.when((oj != j) | (ot != t))
+        def _():
+            for p in range(pols):
+                volt_copy(c, p, ot, oj).wait_send()
+
+    over_channels(first, wait_chirp)
+    over_channels(first, wait_volt)
+
+    @pl.when(active)
+    def _():
+        def wait_power(i, carry):
+            power_copy(lax.rem(me + i, devices)).wait_send()
+            return carry
+
+        lax.fori_loop(1, devices, wait_power, 0)
+
+
+def fused(shift, weights, volt, chirp, tm_count, grp_count, groups):
+    chans, pols, _, rows, f = volt.shape
+    devices = tm_count * grp_count
+    t_rows = f // 2 // devices
+    smem = pl.BlockSpec(memory_space=pltpu.SMEM)
+    hbm = pl.BlockSpec(memory_space=pl.ANY)
+    dma = pltpu.SemaphoreType.DMA
+    square = lambda kind, scale=1: pltpu.VMEM((scale * f, scale * f), kind)
+    return pl.pallas_call(
+        functools.partial(fused_kernel, tm_count=tm_count, grp_count=grp_count, tile=f // 2),
+        out_shape=jax.ShapeDtypeStruct((groups, t_rows, f), f32),
+        in_specs=[smem, smem] + [hbm] * 8,
+        out_specs=pl.BlockSpec(memory_space=pltpu.VMEM),
+        scratch_shapes=[
+            pltpu.VMEM((pols, 2, f, f), bf16),
+            square(f32),
+            pltpu.VMEM((chans, t_rows, f), f32),
+            pltpu.VMEM((f // 2, f), f32),
+            *[square(bf16, 2)] * 4,
+            *[square(f32)] * 4,
+            pltpu.VMEM((2 * f, f), bf16),
+            pltpu.VMEM((2 * f, f), bf16),
+            dma((6,)),
+            dma((pols, chans)),
+            dma((pols,)),
+            dma((chans,)),
+            dma,
+            dma((devices,)),
+            dma,
+        ],
+        compiler_params=pltpu.CompilerParams(
+            vmem_limit_bytes=56 * 1024 * 1024, collective_id=0, has_side_effects=True
+        ),
+    )(shift, weights, volt, chirp, *(jnp.asarray(t) for t in tables(f)))
+
+
 def on_device(voltages, chirp_phase, intersection, group_of):
     tm_count = lax.axis_size("tm")
     grp_count = lax.axis_size("grp")
@@ -174,6 +384,20 @@
     f = chirp_phase.shape[2]
     rows = local_len // f
     groups = 4
+    member = (group_of[None, :] == jnp.arange(groups, dtype=jnp.int32)[:, None]).astype(f32)
+    shares = member / (2.0 * jnp.sum(member, axis=1, keepdims=True))
+    if staggered(chans, tm_count, grp_count) and rows % 16 == 0 and (f // 2) % (8 * devices) == 0:
+        mine = channel_at(tm_rank, grp_rank)[0]
+        result = fused(
+            lax.dynamic_slice(intersection, (mine,), (1,)),
+            shares.reshape(-1),
+            voltages.reshape(chans, pols, 2, rows, f),
+            chirp_phase,
+            tm_count,
+            grp_count,
+            groups,
+        )
+        return result.reshape(beams, groups, -1)
     owners = np.arange(chans) * devices // chans
     owned = np.zeros(devices, np.int32)
     owned[owners] = np.arange(chans)
@@ -191,9 +415,7 @@
     moved = lax.all_to_all(
         power.reshape(devices, -1), ("tm", "grp"), split_axis=0, concat_axis=0, tiled=True
     )
-    member = (group_of[None, :] == jnp.arange(groups, dtype=jnp.int32)[:, None]).astype(f32)
-    counts = jnp.sum(member, axis=1, keepdims=True)
-    weights = jnp.take(member, owned, axis=1) * active[None, :] / (2.0 * counts)
+    weights = jnp.take(shares, owned, axis=1) * active[None, :]
     result = jnp.sum(weights[:, :, None] * moved[None], axis=1)
     return result[None]
 

time: 151 us -> 101 us (0.67); the launches traced: 151 us -> 98.9 us
  waiting for transfers between devices: 74.4 us -> 0 us
  Pallas kernels: 31.6 us -> 90.3 us
  local copies, waits for them, and re-layouts: 22.6 us -> 7.14 us
  starting transfers between devices: 15.4 us -> 0 us
  other arithmetic: 4.47 us -> 1.5 us
  between operations: 2.07 us -> 0.01 us
    all_to_all x3 -> x0, waiting for transfers between devices: 74.4 us -> none  [the longest x1 44.7 us: on_device(): lax.all_to_all(out, ('tm', 'grp'), split_axis=0, concat_axis=0, tiled=True)]
    pallas_call x1, Pallas kernels: 31.6 us -> 90.3 us  [fused(): pl.pallas_call(functools.partial(fused_kernel, tm_count=tm_count, grp_cou...]
    all_to_all x3 -> x0, starting transfers between devices: 15.4 us -> none  [the longest x1 7.43 us: on_device(): lax.all_to_all(out, ('tm', 'grp'), split_axis=0, concat_axis=0, tiled=True)]
    gather x3 -> x0, local copies, waits for them, and re-layouts: 9.89 us -> none  [the longest x1 7.7 us: on_device(): out = jnp.take(voltages[0], owned, axis=0)]
    all_to_all x1 -> x0, local copies, waits for them, and re-layouts: 2.48 us -> none  [on_device(): lax.all_to_all(power.reshape(devices, -1), ('tm', 'grp'), split_axis=0, c...]
    select_n x2 -> x0, other arithmetic: 2.45 us -> none  [on_device(): jnp.take(chirp_phase, column, axis=0)]
    reshape x2, local copies, waits for them, and re-layouts: 7.61 us -> 5.33 us  [the longest x1 3.81 us: on_device(): voltages.reshape(chans, pols, 2, rows, f)]
  transfers between devices with their start and end apart: 3 -> 0, of which waited for: 3 -> 0; matrix products, arithmetic and copies ran while one was open for 9% -> 0% of each run, Pallas kernels for 0% -> 0%
where the time goes in v2:
time: 101 us; the launch traced here: 98.9 us
  Pallas kernels  90.3 us (89%)
  local copies, waits for them, and re-layouts  7.14 us (7%)
  other arithmetic  1.5 us (1%)
    pallas_call x1, Pallas kernels, fused(): pl.pallas_call(functools.partial(fused_kernel, tm_count=tm_count, grp_cou...  90.3 us
    reshape x1, local copies, waits for them, and re-layouts, on_device(): voltages.reshape(chans, pols, 2, rows, f)  3.81 us

profile of v2, /device:TPU:0, one launch (start us, length us, event | category | flops | bytes accessed | tf_op | source)
XLA Modules:
  0.0 98.9 jit_solution(3241498069581529355)
XLA Ops:
  0.0 1.2 %dynamic_slice.3.shift = s32[1]{0:T(128)} dynamic-slice(s32[24]{0:T(128)} %param.12, s32[]{:T(128)S(6)} %select_n.3), dynamic_slice_sizes={1} | dynamic-slice | bytes 12 | tf_op jit(solution)/shard_map/dynamic_slice | solution.py:392
  1.2 0.8 convert_reduce_fusion
  2.0 0.7 convert_divide_fusion
  2.7 0.6 div.52.weights
  3.3 3.8 %reshape.18.volt = bf16[24,2,2,16,512]{4,3,2,1,0:T(8,128)(2,1)} reshape(bf16[1,24,2,2,8192]{4,3,2,1,0:T(2,128)(2,1)} %param.10) | data formatting | bytes 3145728 | tf_op jit(solution)/shard_map/reshape | solution.py:394
  7.1 90.3 %shard_map.100 = f32[4,8,512]{2,1,0:T(8,128)} custom-call(s32[1]{0:T(128)} %dynamic_slice.3.shift, f32[96]{0:T(128)} %div.52.weights, bf16[24,2,2,16,512]{4,3,2,1,0:T(8,128)(2,1)} %reshape.18.volt, f32[24,64,512]{2,1,0:T(8,128)} %chirp.1, bf16[1024,1024]{1,0:T(8,128)(2,1)} %constant.43.clone.h_g2h, bf16[1024,1024]{1,0:T(8,128)(2,1)} %constant.44.clone.h_g2l, ...), custom_call_target="tpu_custom_call" | custom-call | tf_op jit(solution)/shard_map/pallas_call | solution.py:348
  97.4 1.5 %reshape.19 = f32[1,4,4096]{2,1,0:T(4,128)} reshape(f32[4,8,512]{2,1,0:T(8,128)} %shard_map.100) | data formatting | bytes 131072 | tf_op jit(solution)/shard_map/reshape | solution.py:400
  (1 shorter events, 0.0 us)

commit v3 on v2

--- a/solution.py
+++ b/solution.py
@@ -71,6 +71,20 @@
     ramp = (rows * shift + f * ((cols * shift) & (f - 1))) & (nfft - 1)
     turns = phase * (0.5 / math.pi) + ramp.astype(f32) * (1.0 / nfft)
     rest = turns - jnp.round(turns)
+    q = rest * rest
+    cos_fit, sin_fit = turn_polynomials()
+    scale = 1.0 / nfft
+    return horner(q, cos_fit) * scale, horner(q, sin_fit) * (rest * scale)
+
+
+def turn_tables(shift, fraction, k1):
+    f = fraction.shape[1]
+    nfft = f * f
+    rows = k1 + lax.broadcasted_iota(jnp.int32, fraction.shape, 0)
+    cols = lax.broadcasted_iota(jnp.int32, fraction.shape, 1)
+    ramp = rows * shift + f * ((cols * shift) & (f - 1))
+    steps = fraction.astype(jnp.int32) * (nfft // 65536) + ramp
+    rest = (((steps + nfft // 2) & (nfft - 1)) - nfft // 2).astype(f32) * (1.0 / nfft)
     q = rest * rest
     cos_fit, sin_fit = turn_polynomials()
     scale = 1.0 / nfft
@@ -182,9 +196,9 @@
 
 
 def fused_kernel(
-    shift, weights, volt, chirp, h_g2h, h_g2l, h_g3h, h_g3l, h_tc, h_ts, out,
-    z, phase, gathered, power, g2h, g2l, g3h, g3l, tc, ts, cc, cs, vh, vl,
-    table_sem, volt_send, volt_recv, chirp_send, chirp_recv, power_send, power_recv,
+    shifts, group_of, volt, chirp, h_g2h, h_g2l, h_g3h, h_g3l, h_tc, h_ts, out,
+    rows32, rows16, z, phase, gathered, power, g2h, g2l, g3h, g3l, tc, ts, cc, cs, vh, vl,
+    table_sem, rows_sem, volt_send, volt_recv, chirp_send, chirp_recv, power_send, power_recv,
     *, tm_count, grp_count, tile,
 ):
     t, j = lax.axis_index("tm"), lax.axis_index("grp")
@@ -200,6 +214,22 @@
     for load in loads:
         load.start()
 
+    def over_column(act):
+        def step(i, carry):
+            c, owned = channel_at(i, j)
+
+            @pl.when(owned)
+            def _():
+                act(i, c)
+
+            return carry
+
+        lax.fori_loop(0, tm_count, step, 0)
+
+    def load_rows(i, c):
+        return pltpu.make_async_copy(chirp.at[c], rows32.at[i], rows_sem.at[i])
+
+    over_column(lambda i, c: load_rows(i, c).start())
     barrier = pltpu.get_barrier_semaphore()
 
     def greet(i, carry):
@@ -216,10 +246,10 @@
     z_slot = pl.ds(pl.multiple_of(me * rows, rows), rows)
     first = 3 * t
 
-    def chirp_copy(c, ot, oj):
+    def chirp_copy(i):
         return pltpu.make_async_remote_copy(
-            src_ref=chirp.at[c], dst_ref=phase.at[k_slot], send_sem=chirp_send.at[c],
-            recv_sem=chirp_recv, device_id=(ot, oj), device_id_type=MESH,
+            src_ref=rows16.at[i], dst_ref=phase.at[k_slot], send_sem=chirp_send.at[i],
+            recv_sem=chirp_recv, device_id=(i, j), device_id_type=MESH,
         )
 
     def volt_copy(c, p, ot, oj):
@@ -237,32 +267,47 @@
 
         lax.fori_loop(0, chans, step, 0)
 
-    def send_chirp(c, ot, oj):
-        @pl.when((oj == j) & (ot != t))
+    def elsewhere(ot, oj):
+        return (oj != j) | (ot != t)
+
+    def send_first(c, ot, oj):
+        @pl.when(elsewhere(ot, oj))
         def _():
-            chirp_copy(c, ot, oj).start()
-
-    over_channels(first, send_chirp)
+            volt_copy(c, 0, ot, oj).start()
+
+    over_channels(first, send_first)
 
     @pl.when(active)
     def _():
-        pltpu.make_async_copy(chirp.at[mine], phase.at[k_slot], chirp_recv).start()
-
-    def send_pol(p, carry):
-        def send_volt(c, ot, oj):
-            @pl.when((oj != j) | (ot != t))
+        def own(p, carry):
+            pltpu.make_async_copy(volt.at[mine, p], z.at[p, :, z_slot], volt_recv.at[p]).start()
+            return carry
+
+        lax.fori_loop(0, pols, own, 0)
+
+    def send_rows(i, c):
+        load_rows(i, c).wait()
+        rows16[i] = jnp.round(rows32[i] * (32768.0 / math.pi)).astype(jnp.int32).astype(jnp.int16)
+
+        @pl.when(i != t)
+        def _():
+            chirp_copy(i).start()
+
+        @pl.when(i == t)
+        def _():
+            pltpu.make_async_copy(rows16.at[i], phase.at[k_slot], chirp_recv).start()
+
+    over_column(send_rows)
+
+    for p in range(1, pols):
+        def send_next(c, ot, oj):
+            @pl.when(elsewhere(ot, oj))
             def _():
+                volt_copy(c, p - 1, ot, oj).wait_send()
                 volt_copy(c, p, ot, oj).start()
 
-        over_channels(first, send_volt)
-
-        @pl.when(active)
-        def _():
-            pltpu.make_async_copy(volt.at[mine, p], z.at[p, :, z_slot], volt_recv.at[p]).start()
-
-        return carry
-
-    lax.fori_loop(0, pols, send_pol, 0)
+        over_channels(first, send_next)
+
     for load in loads:
         load.wait()
 
@@ -279,7 +324,7 @@
 
         def chirp_step(i, carry):
             part = pl.ds(pl.multiple_of(i * 64, 64), 64)
-            cc[part], cs[part] = chirp_tables(shift[0], phase[part], i * 64)
+            cc[part], cs[part] = turn_tables(shifts[mine], phase[part], i * 64)
             return carry
 
         lax.fori_loop(0, f // 64, chirp_step, 0)
@@ -309,23 +354,27 @@
 
     pltpu.make_async_copy(gathered, gathered, power_recv).wait()
     for g in range(out.shape[0]):
-        total = weights[g * chans] * gathered[0]
-        for c in range(1, chans):
-            total = total + weights[g * chans + c] * gathered[c]
-        out[g] = total
-
-    def wait_chirp(c, ot, oj):
-        @pl.when((oj == j) & (ot != t))
+        total = jnp.zeros((t_rows, f), f32)
+        count = jnp.int32(0)
+        for c in range(chans):
+            member = (group_of[c] == g).astype(jnp.int32)
+            count = count + member
+            total = total + member.astype(f32) * gathered[c]
+        total = total / jnp.full((t_rows, f), 2 * count, jnp.int32).astype(f32)
+        for r in range(t_rows):
+            out[g : g + 1, r * f : (r + 1) * f] = total[r : r + 1]
+
+    def wait_rows(i, c):
+        @pl.when(i != t)
         def _():
-            chirp_copy(c, ot, oj).wait_send()
+            chirp_copy(i).wait_send()
 
     def wait_volt(c, ot, oj):
-        @pl.when((oj != j) | (ot != t))
+        @pl.when(elsewhere(ot, oj))
         def _():
-            for p in range(pols):
-                volt_copy(c, p, ot, oj).wait_send()
-
-    over_channels(first, wait_chirp)
+            volt_copy(c, pols - 1, ot, oj).wait_send()
+
+    over_column(wait_rows)
     over_channels(first, wait_volt)
 
     @pl.when(active)
@@ -337,7 +386,7 @@
         lax.fori_loop(1, devices, wait_power, 0)
 
 
-def fused(shift, weights, volt, chirp, tm_count, grp_count, groups):
+def fused(shifts, group_of, volt, chirp, tm_count, grp_count, groups):
     chans, pols, _, rows, f = volt.shape
     devices = tm_count * grp_count
     t_rows = f // 2 // devices
@@ -347,12 +396,14 @@
     square = lambda kind, scale=1: pltpu.VMEM((scale * f, scale * f), kind)
     return pl.pallas_call(
         functools.partial(fused_kernel, tm_count=tm_count, grp_count=grp_count, tile=f // 2),
-        out_shape=jax.ShapeDtypeStruct((groups, t_rows, f), f32),
+        out_shape=jax.ShapeDtypeStruct((groups, t_rows * f), f32),
         in_specs=[smem, smem] + [hbm] * 8,
         out_specs=pl.BlockSpec(memory_space=pltpu.VMEM),
         scratch_shapes=[
+            pltpu.VMEM((tm_count, chirp.shape[1], f), f32),
+            pltpu.VMEM((tm_count, chirp.shape[1], f), jnp.int16),
             pltpu.VMEM((pols, 2, f, f), bf16),
-            square(f32),
+            square(jnp.int16),
             pltpu.VMEM((chans, t_rows, f), f32),
             pltpu.VMEM((f // 2, f), f32),
             *[square(bf16, 2)] * 4,
@@ -360,9 +411,10 @@
             pltpu.VMEM((2 * f, f), bf16),
             pltpu.VMEM((2 * f, f), bf16),
             dma((6,)),
+            dma((tm_count,)),
             dma((pols, chans)),
             dma((pols,)),
-            dma((chans,)),
+            dma((tm_count,)),
             dma,
             dma((devices,)),
             dma,
@@ -370,7 +422,7 @@
         compiler_params=pltpu.CompilerParams(
             vmem_limit_bytes=56 * 1024 * 1024, collective_id=0, has_side_effects=True
         ),
-    )(shift, weights, volt, chirp, *(jnp.asarray(t) for t in tables(f)))
+    )(shifts, group_of, volt, chirp, *(jnp.asarray(t) for t in tables(f)))
 
 
 def on_device(voltages, chirp_phase, intersection, group_of):
@@ -386,11 +438,11 @@
     groups = 4
     member = (group_of[None, :] == jnp.arange(groups, dtype=jnp.int32)[:, None]).astype(f32)
     shares = member / (2.0 * jnp.sum(member, axis=1, keepdims=True))
-    if staggered(chans, tm_count, grp_count) and rows % 16 == 0 and (f // 2) % (8 * devices) == 0:
-        mine = channel_at(tm_rank, grp_rank)[0]
+    whole_tiles = rows % 16 == 0 and chirp_phase.shape[1] % 16 == 0 and (f // 2) % (8 * devices) == 0
+    if staggered(chans, tm_count, grp_count) and whole_tiles and f * f % 65536 == 0:
         result = fused(
-            lax.dynamic_slice(intersection, (mine,), (1,)),
-            shares.reshape(-1),
+            intersection,
+            group_of,
             voltages.reshape(chans, pols, 2, rows, f),
             chirp_phase,
             tm_count,

time: 101 us -> 85.1 us (0.84)
  Pallas kernels: 90.3 us -> 78.7 us
  local copies, waits for them, and re-layouts: 7.14 us -> 5.29 us
  other arithmetic: 1.5 us -> 0 us
    pallas_call x1, Pallas kernels: 90.3 us -> 78.7 us  [fused(): pl.pallas_call(functools.partial(fused_kernel, tm_count=tm_count, grp_cou...]
    reshape x1 -> x0, local copies, waits for them, and re-layouts: 1.52 us -> none  [on_device(): return result.reshape(beams, groups, -1)]
    unnamed x0 -> x1, local copies, waits for them, and re-layouts: none -> 1.47 us
    dynamic_slice x1 -> x0, local copies, waits for them, and re-layouts: 1.24 us -> none  [on_device(): lax.dynamic_slice(intersection, (mine,), (1,))]
where the time goes in v3:
time: 85.1 us; the launch traced here: 84 us
  Pallas kernels  78.7 us (92%)
  local copies, waits for them, and re-layouts  5.29 us (6%)
    pallas_call x1, Pallas kernels, fused(): pl.pallas_call(functools.partial(fused_kernel, tm_count=tm_count, grp_cou...  78.7 us
    reshape x1, local copies, waits for them, and re-layouts, on_device(): voltages.reshape(chans, pols, 2, rows, f)  3.81 us

profile of v3, /device:TPU:0, one launch (start us, length us, event | category | flops | bytes accessed | tf_op | source)
XLA Modules:
  0.0 84.0 jit_solution(9409593443859270787)
XLA Ops:
  0.0 3.8 %reshape.6.volt = bf16[24,2,2,16,512]{4,3,2,1,0:T(8,128)(2,1)} reshape(bf16[1,24,2,2,8192]{4,3,2,1,0:T(2,128)(2,1)} %param.10) | data formatting | bytes 3145728 | tf_op jit(solution)/shard_map/reshape | solution.py:446
  3.8 78.7 %shard_map.100 = f32[4,4096]{1,0:T(4,128)} custom-call(s32[24]{0:T(128)} %shifts.1, s32[24]{0:T(128)} %group_of.1, bf16[24,2,2,16,512]{4,3,2,1,0:T(8,128)(2,1)} %reshape.6.volt, f32[24,64,512]{2,1,0:T(8,128)} %chirp.1, bf16[1024,1024]{1,0:T(8,128)(2,1)} %constant.12.clone.h_g2h, bf16[1024,1024]{1,0:T(8,128)(2,1)} %constant.13.clone.h_g2l, ...), custom_call_target="tpu_custom_call" | custom-call | tf_op jit(solution)/shard_map/pallas_call | solution.py:397
  82.5 1.5 %copy.12 = f32[1,4,4096]{2,1,0:T(4,128)} copy(f32[1,4,4096]{2,1,0:T(4,128)} %bitcast.1) | data formatting | bytes 131072

commit v4 on v3

--- a/solution.py
+++ b/solution.py
@@ -24,21 +24,34 @@
     return np.asarray(high), np.asarray(low)
 
 
+def halves(c, s, sign):
+    return np.block([[c, sign * s], [-sign * s, c]])
+
+
 @functools.lru_cache(None)
 def tables(f):
+    h = f // 2
     index = np.arange(f)
     product = index[:, None] * index[None, :]
     angle = 2.0 * np.pi * (product % f) / f
     c, s = np.cos(angle), np.sin(angle)
-    forward = np.block([[c, -s], [s, c]])
-    inverse = np.block([[c, s], [-s, c]])
+    left = np.stack(np_split(np.block([[c, s], [-s, c]])))
+    ahead, back, last = [], [], []
+    for odd in (0, 1):
+        ahead.append(np.stack(np_split(halves(c[:h, odd::2], s[:h, odd::2], -1))))
+        back.append(np.stack(np_split(halves(c[odd::2, :h], s[odd::2, :h], 1))))
+        part = slice(odd, h, 2)
+        last.append(np.stack(np_split(np.block([[c[part, :h], -s[part, :h]], [s[part, :h], c[part, :h]]]))))
     twist = 2.0 * np.pi * product / (f * f)
-    return (
-        *np_split(forward),
-        *np_split(inverse),
-        np.cos(twist).astype(np.float32),
-        np.sin(twist).astype(np.float32),
-    )
+    turned = np.stack([np.cos(twist), np.sin(twist)]).astype(np.float32)
+    order = np.eye(f)[:, np.concatenate([index[::2], index[1::2]])].astype(bf16)
+    return left, np.stack(ahead), np.stack(back), np.stack(last), turned, np.asarray(order)
+
+
+def column_ids(shape):
+    h = shape[1] // 2
+    cols = lax.broadcasted_iota(jnp.int32, shape, 1)
+    return 2 * (cols & (h - 1)) + (cols >= h).astype(jnp.int32)
 
 
 @functools.lru_cache(None)
@@ -67,7 +80,7 @@
     f = phase.shape[1]
     nfft = f * f
     rows = k1 + lax.broadcasted_iota(jnp.int32, phase.shape, 0)
-    cols = lax.broadcasted_iota(jnp.int32, phase.shape, 1)
+    cols = column_ids(phase.shape)
     ramp = (rows * shift + f * ((cols * shift) & (f - 1))) & (nfft - 1)
     turns = phase * (0.5 / math.pi) + ramp.astype(f32) * (1.0 / nfft)
     rest = turns - jnp.round(turns)
@@ -77,13 +90,18 @@
     return horner(q, cos_fit) * scale, horner(q, sin_fit) * (rest * scale)
 
 
-def turn_tables(shift, fraction, k1):
+def turn_tables(shift, fraction, order, k1):
+    whole = fraction.astype(jnp.int32)
+    upper = whole >> 8
+    parts = jnp.concatenate([upper, whole - upper * 256], axis=0).astype(f32).astype(bf16)
+    moved = mm(parts, order).astype(jnp.int32)
+    fraction = moved[: whole.shape[0]] * 256 + moved[whole.shape[0] :]
     f = fraction.shape[1]
     nfft = f * f
     rows = k1 + lax.broadcasted_iota(jnp.int32, fraction.shape, 0)
-    cols = lax.broadcasted_iota(jnp.int32, fraction.shape, 1)
+    cols = column_ids(fraction.shape)
     ramp = rows * shift + f * ((cols * shift) & (f - 1))
-    steps = fraction.astype(jnp.int32) * (nfft // 65536) + ramp
+    steps = fraction * (nfft // 65536) + ramp
     rest = (((steps + nfft // 2) & (nfft - 1)) - nfft // 2).astype(f32) * (1.0 / nfft)
     q = rest * rest
     cos_fit, sin_fit = turn_polynomials()
@@ -102,38 +120,49 @@
     return both[:rows] + both[rows:] + mm(vh, low)
 
 
-def rows_step(i, z, g2h, g2l, g3h, g3l, tc, ts, cc, cs, vh, vl, tile):
-    f = tc.shape[0]
+def rows_step(i, z, left, ahead, back, turned, cc, cs, v, tile):
+    f = cc.shape[0]
+    h = f // 2
     top = pl.ds(pl.multiple_of(i * tile, tile), tile)
     bot = pl.ds(pl.multiple_of(f + i * tile, tile), tile)
-    lhs = jnp.concatenate([g3h[top], g3h[bot], g3l[top], g3l[bot]], axis=0)
+    lhs = jnp.concatenate([left[0, top], left[0, bot], left[1, top], left[1, bot]], axis=0)
     r = mm(lhs, z)
     yr = r[:tile] + r[2 * tile : 3 * tile]
     yi = r[tile : 2 * tile] + r[3 * tile :]
-    c, s = tc[top], ts[top]
-    spec = three(jnp.concatenate([yr * c + yi * s, yi * c - yr * s], axis=1), g2h[...], g2l[...])
-    zr, zi = spec[:, :f], spec[:, f:]
-    hc, hs = cc[top], cs[top]
-    v = three(jnp.concatenate([zr * hc - zi * hs, zr * hs + zi * hc], axis=1), g3h[...], g3l[...])
-    vr, vi = v[:, :f], v[:, f:]
-    ah, al = split(vr * c - vi * s)
-    vh[top], vl[top] = ah, al
-    ah, al = split(vr * s + vi * c)
-    vh[bot], vl[bot] = ah, al
-
-
-def last_step(g2h, g2l, vh, vl):
-    f = vh.shape[1]
-    half = f // 2
-    highs = [g2h[:half], g2h[f : f + half]]
-    lhs = jnp.concatenate(highs + [g2l[:half], g2l[f : f + half]], axis=0)
-    r = mm(lhs, vh[...])
-    sig = r[:f] + r[f:] + mm(jnp.concatenate(highs, axis=0), vl[...])
-    sr, si = sig[:half], sig[half:]
-    return sr * sr + si * si
-
-
-def local_kernel(shift, z, phase, g2h, g2l, g3h, g3l, tc, ts, power, cc, cs, vh, vl, *, tile):
+    c, s = turned[0, top], turned[1, top]
+    ar, ai = yr * c + yi * s, yi * c - yr * s
+    found = []
+    for odd in (0, 1):
+        sign = 1 - 2 * odd
+        pair = [ar[:, :h] + sign * ar[:, h:], ai[:, :h] + sign * ai[:, h:]]
+        spec = three(jnp.concatenate(pair, axis=1), ahead[odd, 0], ahead[odd, 1])
+        zr, zi = spec[:, :h], spec[:, h:]
+        cols = slice(odd * h, (odd + 1) * h)
+        hc, hs = cc[top, cols], cs[top, cols]
+        pair = [zr * hc - zi * hs, zr * hs + zi * hc]
+        found.append(three(jnp.concatenate(pair, axis=1), back[odd, 0], back[odd, 1]))
+    plus, minus = found[0] + found[1], found[0] - found[1]
+    vr = jnp.concatenate([plus[:, :h], minus[:, :h]], axis=1)
+    vi = jnp.concatenate([plus[:, h:], minus[:, h:]], axis=1)
+    v[top] = vr * c - vi * s
+    v[bot] = vr * s + vi * c
+
+
+def last_step(last, v, power):
+    f = v.shape[1]
+    h, q = f // 2, f // 4
+    for odd in (0, 1):
+        sign = 1 - 2 * odd
+        both = [v[:h] + sign * v[h:f], v[f : f + h] + sign * v[f + h :]]
+        vh, vl = split(jnp.concatenate(both, axis=0))
+        high, low = last[odd, 0], last[odd, 1]
+        r = mm(jnp.concatenate([high, low], axis=0), vh)
+        sig = r[:h] + r[h:] + mm(high, vl)
+        sr, si = sig[:q], sig[q:]
+        power[odd] += sr * sr + si * si
+
+
+def local_kernel(shift, z, phase, left, ahead, back, last, turned, order, power, cc, cs, v, *, tile):
     f = phase.shape[0]
     pols = z.shape[0]
 
@@ -147,11 +176,11 @@
 
     def pol_step(p, carry):
         def step(i, inner):
-            rows_step(i, z[p], g2h, g2l, g3h, g3l, tc, ts, cc, cs, vh, vl, tile)
+            rows_step(i, z[p], left, ahead, back, turned, cc, cs, v, tile)
             return inner
 
         lax.fori_loop(0, f // tile, step, 0)
-        power[...] += last_step(g2h, g2l, vh, vl)
+        last_step(last, v, power)
         return carry
 
     lax.fori_loop(0, pols, pol_step, 0)
@@ -162,19 +191,20 @@
     tile = f // 2
     smem = pl.BlockSpec(memory_space=pltpu.SMEM)
     vmem = pl.BlockSpec(memory_space=pltpu.VMEM)
-    return pl.pallas_call(
+    phase = jnp.concatenate([phase[:, ::2], phase[:, 1::2]], axis=1)
+    power = pl.pallas_call(
         functools.partial(local_kernel, tile=tile),
-        out_shape=jax.ShapeDtypeStruct((f // 2, f), f32),
+        out_shape=jax.ShapeDtypeStruct((2, f // 4, f), f32),
         in_specs=[smem] + [vmem] * 8,
         out_specs=vmem,
         scratch_shapes=[
             pltpu.VMEM((f, f), f32),
             pltpu.VMEM((f, f), f32),
-            pltpu.VMEM((2 * f, f), bf16),
-            pltpu.VMEM((2 * f, f), bf16),
+            pltpu.VMEM((2 * f, f), f32),
         ],
         compiler_params=pltpu.CompilerParams(vmem_limit_bytes=56 * 1024 * 1024),
     )(shift, z, phase, *(jnp.asarray(t) for t in tables(f)))
+    return jnp.swapaxes(power, 0, 1).reshape(f // 2, f)
 
 
 MESH = pl.DeviceIdType.MESH
@@ -196,8 +226,8 @@
 
 
 def fused_kernel(
-    shifts, group_of, volt, chirp, h_g2h, h_g2l, h_g3h, h_g3l, h_tc, h_ts, out,
-    rows32, rows16, z, phase, gathered, power, g2h, g2l, g3h, g3l, tc, ts, cc, cs, vh, vl,
+    shifts, group_of, volt, chirp, h_left, h_ahead, h_back, h_last, h_turned, h_order, out,
+    rows32, rows16, z, phase, gathered, summed, power, left, ahead, back, last, turned, order, cc, cs, v,
     table_sem, rows_sem, volt_send, volt_recv, chirp_send, chirp_recv, power_send, power_recv,
     *, tm_count, grp_count, tile,
 ):
@@ -209,7 +239,8 @@
     t_rows = gathered.shape[1]
     mine, active = channel_at(t, j)
 
-    pairs = [(h_g2h, g2h), (h_g2l, g2l), (h_g3h, g3h), (h_g3l, g3l), (h_tc, tc), (h_ts, ts)]
+    pairs = [(h_left, left), (h_ahead, ahead), (h_back, back)]
+    pairs += [(h_last, last), (h_turned, turned), (h_order, order)]
     loads = [pltpu.make_async_copy(a, b, table_sem.at[i]) for i, (a, b) in enumerate(pairs)]
     for load in loads:
         load.start()
@@ -313,7 +344,7 @@
 
     def power_copy(d):
         return pltpu.make_async_remote_copy(
-            src_ref=power.at[pl.ds(pl.multiple_of(d * t_rows, t_rows), t_rows)],
+            src_ref=power.at[d],
             dst_ref=gathered.at[mine], send_sem=power_send.at[d], recv_sem=power_recv,
             device_id=(lax.div(d, grp_count), lax.rem(d, grp_count)), device_id_type=MESH,
         )
@@ -324,33 +355,37 @@
 
         def chirp_step(i, carry):
             part = pl.ds(pl.multiple_of(i * 64, 64), 64)
-            cc[part], cs[part] = turn_tables(shifts[mine], phase[part], i * 64)
+            cc[part], cs[part] = turn_tables(shifts[mine], phase[part], order[...], i * 64)
             return carry
 
         lax.fori_loop(0, f // 64, chirp_step, 0)
-        power[...] = jnp.zeros_like(power)
+        summed[...] = jnp.zeros_like(summed)
 
         def pol_step(p, carry):
             pltpu.make_async_copy(z.at[p], z.at[p], volt_recv.at[p]).wait()
 
             def step(i, inner):
                 samples = z[p].reshape(2 * f, f)
-                rows_step(i, samples, g2h, g2l, g3h, g3l, tc, ts, cc, cs, vh, vl, tile)
+                rows_step(i, samples, left, ahead, back, turned, cc, cs, v, tile)
                 return inner
 
             lax.fori_loop(0, f // tile, step, 0)
-            power[...] += last_step(g2h, g2l, vh, vl)
+            last_step(last, v, summed)
             return carry
 
         lax.fori_loop(0, pols, pol_step, 0)
+
+        q = t_rows // 2
+        for d in range(devices):
+            for odd in (0, 1):
+                power[d, odd * q : (odd + 1) * q] = summed[odd, d * q : (d + 1) * q]
 
         def send_power(i, carry):
             power_copy(lax.rem(me + i, devices)).start()
             return carry
 
         lax.fori_loop(1, devices, send_power, 0)
-        own = power.at[pl.ds(pl.multiple_of(me * t_rows, t_rows), t_rows)]
-        pltpu.make_async_copy(own, gathered.at[mine], power_recv).start()
+        pltpu.make_async_copy(power.at[me], gathered.at[mine], power_recv).start()
 
     pltpu.make_async_copy(gathered, gathered, power_recv).wait()
     for g in range(out.shape[0]):
@@ -362,7 +397,8 @@
             total = total + member.astype(f32) * gathered[c]
         total = total / jnp.full((t_rows, f), 2 * count, jnp.int32).astype(f32)
         for r in range(t_rows):
-            out[g : g + 1, r * f : (r + 1) * f] = total[r : r + 1]
+            when = 2 * r if r < t_rows // 2 else 2 * r - t_rows + 1
+            out[g : g + 1, when * f : (when + 1) * f] = total[r : r + 1]
 
     def wait_rows(i, c):
         @pl.when(i != t)
@@ -393,7 +429,7 @@
     smem = pl.BlockSpec(memory_space=pltpu.SMEM)
     hbm = pl.BlockSpec(memory_space=pl.ANY)
     dma = pltpu.SemaphoreType.DMA
-    square = lambda kind, scale=1: pltpu.VMEM((scale * f, scale * f), kind)
+    square = lambda kind: pltpu.VMEM((f, f), kind)
     return pl.pallas_call(
         functools.partial(fused_kernel, tm_count=tm_count, grp_count=grp_count, tile=f // 2),
         out_shape=jax.ShapeDtypeStruct((groups, t_rows * f), f32),
@@ -405,11 +441,12 @@
             pltpu.VMEM((pols, 2, f, f), bf16),
             square(jnp.int16),
             pltpu.VMEM((chans, t_rows, f), f32),
-            pltpu.VMEM((f // 2, f), f32),
-            *[square(bf16, 2)] * 4,
-            *[square(f32)] * 4,
-            pltpu.VMEM((2 * f, f), bf16),
-            pltpu.VMEM((2 * f, f), bf16),
+            pltpu.VMEM((2, f // 4, f), f32),
+            pltpu.VMEM((devices, t_rows, f), f32),
+            *[pltpu.VMEM(t.shape, t.dtype) for t in tables(f)],
+            square(f32),
+            square(f32),
+            pltpu.VMEM((2 * f, f), f32),
             dma((6,)),
             dma((tm_count,)),
             dma((pols, chans)),

time: 85.1 us -> 78.8 us (0.926)
  Pallas kernels: 78.7 us -> 72.4 us
    pallas_call x1, Pallas kernels: 78.7 us -> 72.4 us  [fused(): pl.pallas_call(functools.partial(fused_kernel, tm_count=tm_count, grp_cou...]
where the time goes in v4:
time: 78.8 us; the launch traced here: 77.7 us
  Pallas kernels  72.4 us (92%)
  local copies, waits for them, and re-layouts  5.29 us (7%)
    pallas_call x1, Pallas kernels, fused(): pl.pallas_call(functools.partial(fused_kernel, tm_count=tm_count, grp_cou...  72.4 us
    reshape x1, local copies, waits for them, and re-layouts, on_device(): voltages.reshape(chans, pols, 2, rows, f)  3.81 us

profile of v4, /device:TPU:0, one launch (start us, length us, event | category | flops | bytes accessed | tf_op | source)
XLA Modules:
  0.0 77.7 jit_solution(7526460321613252611)
XLA Ops:
  0.0 3.8 %reshape.6.volt = bf16[24,2,2,16,512]{4,3,2,1,0:T(8,128)(2,1)} reshape(bf16[1,24,2,2,8192]{4,3,2,1,0:T(2,128)(2,1)} %param.10) | data formatting | bytes 3145728 | tf_op jit(solution)/shard_map/reshape | solution.py:483
  3.8 72.4 %shard_map.100 = f32[4,4096]{1,0:T(4,128)} custom-call(s32[24]{0:T(128)} %shifts.1, s32[24]{0:T(128)} %group_of.1, bf16[24,2,2,16,512]{4,3,2,1,0:T(8,128)(2,1)} %reshape.6.volt, f32[24,64,512]{2,1,0:T(8,128)} %chirp.1, bf16[2,1024,1024]{2,1,0:T(8,128)(2,1)} %constant.12.clone.h_left, bf16[2,2,512,512]{3,2,1,0:T(8,128)(2,1)} %constant.13.clone.h_ahead, ...), custom_call_target="tpu_custom_call" | custom-call | tf_op jit(solution)/shard_map/pallas_call | solution.py:433
  76.2 1.5 %copy.12 = f32[1,4,4096]{2,1,0:T(4,128)} copy(f32[1,4,4096]{2,1,0:T(4,128)} %bitcast.1) | data formatting | bytes 131072

commit v5 on v4

--- a/solution.py
+++ b/solution.py
@@ -227,18 +227,21 @@
 
 def fused_kernel(
     shifts, group_of, volt, chirp, h_left, h_ahead, h_back, h_last, h_turned, h_order, out,
-    rows32, rows16, z, phase, gathered, summed, power, left, ahead, back, last, turned, order, cc, cs, v,
-    table_sem, rows_sem, volt_send, volt_recv, chirp_send, chirp_recv, power_send, power_recv,
+    raw, staged, rows32, rows16, z, phase, gathered, summed, power, left, ahead, back, last, turned, order, cc, cs, v,
+    raw_sem, table_sem, rows_sem, volt_send, volt_recv, chirp_send, chirp_recv, power_send, power_recv,
     *, tm_count, grp_count, tile,
 ):
     t, j = lax.axis_index("tm"), lax.axis_index("grp")
     devices = tm_count * grp_count
     me = t * grp_count + j
-    chans, pols, _, rows, f = volt.shape
+    chans, pols, _, rows, f = staged.shape
     k_rows = chirp.shape[1]
     t_rows = gathered.shape[1]
     mine, active = channel_at(t, j)
 
+    first = 3 * t
+    fetch = pltpu.make_async_copy(volt, raw, raw_sem)
+    fetch.start()
     pairs = [(h_left, left), (h_ahead, ahead), (h_back, back)]
     pairs += [(h_last, last), (h_turned, turned), (h_order, order)]
     loads = [pltpu.make_async_copy(a, b, table_sem.at[i]) for i, (a, b) in enumerate(pairs)]
@@ -271,11 +274,22 @@
         return carry
 
     lax.fori_loop(1, devices, greet, 0)
+
+    def stage(i, p):
+        c = lax.rem(first + i, chans)
+        staged[c, p] = raw[c, p].astype(f32).reshape(2, rows, f).astype(bf16)
+
+    def stage_early(i, carry):
+        stage(i, 0)
+        return carry
+
+    early = chans // 3
+    fetch.wait()
+    lax.fori_loop(0, early, stage_early, 0)
     pl.semaphore_wait(barrier, devices - 1)
 
     k_slot = pl.ds(pl.multiple_of(t * k_rows, k_rows), k_rows)
     z_slot = pl.ds(pl.multiple_of(me * rows, rows), rows)
-    first = 3 * t
 
     def chirp_copy(i):
         return pltpu.make_async_remote_copy(
@@ -285,7 +299,7 @@
 
     def volt_copy(c, p, ot, oj):
         return pltpu.make_async_remote_copy(
-            src_ref=volt.at[c, p], dst_ref=z.at[p, :, z_slot], send_sem=volt_send.at[p, c],
+            src_ref=staged.at[c, p], dst_ref=z.at[p, :, z_slot], send_sem=volt_send.at[p, c],
             recv_sem=volt_recv.at[p], device_id=(ot, oj), device_id_type=MESH,
         )
 
@@ -293,7 +307,7 @@
         def step(i, carry):
             c = lax.rem(start + i, chans)
             ot, oj = owner_of(c)
-            act(c, ot, oj)
+            act(i, c, ot, oj)
             return carry
 
         lax.fori_loop(0, chans, step, 0)
@@ -301,20 +315,23 @@
     def elsewhere(ot, oj):
         return (oj != j) | (ot != t)
 
-    def send_first(c, ot, oj):
+    def send_first(i, c, ot, oj):
         @pl.when(elsewhere(ot, oj))
         def _():
             volt_copy(c, 0, ot, oj).start()
 
+        @pl.when(i + early < chans)
+        def _():
+            stage(i + early, 0)
+
     over_channels(first, send_first)
 
-    @pl.when(active)
-    def _():
-        def own(p, carry):
-            pltpu.make_async_copy(volt.at[mine, p], z.at[p, :, z_slot], volt_recv.at[p]).start()
-            return carry
-
-        lax.fori_loop(0, pols, own, 0)
+    def own(p):
+        @pl.when(active)
+        def _():
+            pltpu.make_async_copy(staged.at[mine, p], z.at[p, :, z_slot], volt_recv.at[p]).start()
+
+    own(0)
 
     def send_rows(i, c):
         load_rows(i, c).wait()
@@ -331,7 +348,14 @@
     over_column(send_rows)
 
     for p in range(1, pols):
-        def send_next(c, ot, oj):
+        def stage_next(i, carry):
+            stage(i, p)
+            return carry
+
+        lax.fori_loop(0, chans, stage_next, 0)
+        own(p)
+
+        def send_next(i, c, ot, oj):
             @pl.when(elsewhere(ot, oj))
             def _():
                 volt_copy(c, p - 1, ot, oj).wait_send()
@@ -405,7 +429,7 @@
         def _():
             chirp_copy(i).wait_send()
 
-    def wait_volt(c, ot, oj):
+    def wait_volt(i, c, ot, oj):
         @pl.when(elsewhere(ot, oj))
         def _():
             volt_copy(c, pols - 1, ot, oj).wait_send()
@@ -423,7 +447,9 @@
 
 
 def fused(shifts, group_of, volt, chirp, tm_count, grp_count, groups):
-    chans, pols, _, rows, f = volt.shape
+    chans, pols, _, local_len = volt.shape
+    f = chirp.shape[2]
+    rows = local_len // f
     devices = tm_count * grp_count
     t_rows = f // 2 // devices
     smem = pl.BlockSpec(memory_space=pltpu.SMEM)
@@ -436,6 +462,8 @@
         in_specs=[smem, smem] + [hbm] * 8,
         out_specs=pl.BlockSpec(memory_space=pltpu.VMEM),
         scratch_shapes=[
+            pltpu.VMEM(volt.shape, bf16),
+            pltpu.VMEM((chans, pols, 2, rows, f), bf16),
             pltpu.VMEM((tm_count, chirp.shape[1], f), f32),
             pltpu.VMEM((tm_count, chirp.shape[1], f), jnp.int16),
             pltpu.VMEM((pols, 2, f, f), bf16),
@@ -447,6 +475,7 @@
             square(f32),
             square(f32),
             pltpu.VMEM((2 * f, f), f32),
+            dma,
             dma((6,)),
             dma((tm_count,)),
             dma((pols, chans)),
@@ -480,7 +509,7 @@
         result = fused(
             intersection,
             group_of,
-            voltages.reshape(chans, pols, 2, rows, f),
+            voltages[0],
             chirp_phase,
             tm_count,
             grp_count,

time: 78.8 us -> 77.9 us (0.989)
  local copies, waits for them, and re-layouts: 5.29 us -> 1.47 us
  Pallas kernels: 72.4 us -> 75.1 us
    reshape x1 -> x0, local copies, waits for them, and re-layouts: 3.81 us -> none  [on_device(): voltages.reshape(chans, pols, 2, rows, f)]
    pallas_call x1, Pallas kernels: 72.4 us -> 75.1 us  [fused(): pl.pallas_call(functools.partial(fused_kernel, tm_count=tm_count, grp_cou...]
where the time goes in v5:
time: 77.9 us; the launch traced here: 76.5 us
  Pallas kernels  75.1 us (96%)
  local copies, waits for them, and re-layouts  1.47 us (2%)
    pallas_call x1, Pallas kernels, fused(): pl.pallas_call(functools.partial(fused_kernel, tm_count=tm_count, grp_cou...  75.1 us

profile of v5, /device:TPU:0, one launch (start us, length us, event | category | flops | bytes accessed | tf_op | source)
XLA Modules:
  0.0 76.5 jit_solution(11887289040742584698)
XLA Ops:
  0.0 75.1 %shard_map.100 = f32[4,4096]{1,0:T(4,128)} custom-call(s32[24]{0:T(128)} %shifts.1, s32[24]{0:T(128)} %group_of.1, bf16[24,2,2,8192]{3,2,1,0:T(2,128)(2,1)} %bitcast.2, f32[24,64,512]{2,1,0:T(8,128)} %chirp.1, bf16[2,1024,1024]{2,1,0:T(8,128)(2,1)} %constant.12.clone.h_left, bf16[2,2,512,512]{3,2,1,0:T(8,128)(2,1)} %constant.13.clone.h_ahead, ...), custom_call_target="tpu_custom_call" | custom-call | tf_op jit(solution)/shard_map/pallas_call | solution.py:459
  75.1 1.5 %copy.12 = f32[1,4,4096]{2,1,0:T(4,128)} copy(f32[1,4,4096]{2,1,0:T(4,128)} %bitcast.3) | data formatting | bytes 131072

commit v6 on v5

--- a/solution.py
+++ b/solution.py
@@ -211,13 +211,19 @@
 
 
 def staggered(chans, tm_count, grp_count):
-    return grp_count == 4 and chans == tm_count * (grp_count - 1)
+    return grp_count == 4 and chans == tm_count * (grp_count - 1) and tm_count % 2 == 0
 
 
 def owner_of(c):
     t, k = lax.div(c, 3), lax.rem(c, 3)
     a = lax.rem(lax.div(t, 2) + lax.rem(t, 2), 2)
     return t, k + a * lax.div(k + 1, 2)
+
+
+def far_first(i, count, t, tm_count, shift=0):
+    per, half = count // 2, tm_count // 2
+    side = lax.rem(lax.div(t, half) + 1 + lax.div(i, per), 2)
+    return side * per + lax.rem(i + lax.rem(t, half) * (count // tm_count) + shift, per)
 
 
 def channel_at(t, j):
@@ -239,7 +245,6 @@
     t_rows = gathered.shape[1]
     mine, active = channel_at(t, j)
 
-    first = 3 * t
     fetch = pltpu.make_async_copy(volt, raw, raw_sem)
     fetch.start()
     pairs = [(h_left, left), (h_ahead, ahead), (h_back, back)]
@@ -249,7 +254,8 @@
         load.start()
 
     def over_column(act):
-        def step(i, carry):
+        def step(turn, carry):
+            i = far_first(turn, tm_count, t, tm_count)
             c, owned = channel_at(i, j)
 
             @pl.when(owned)
@@ -276,7 +282,7 @@
     lax.fori_loop(1, devices, greet, 0)
 
     def stage(i, p):
-        c = lax.rem(first + i, chans)
+        c = far_first(i, chans, t, tm_count)
         staged[c, p] = raw[c, p].astype(f32).reshape(2, rows, f).astype(bf16)
 
     def stage_early(i, carry):
@@ -303,9 +309,9 @@
             recv_sem=volt_recv.at[p], device_id=(ot, oj), device_id_type=MESH,
         )
 
-    def over_channels(start, act):
+    def over_channels(act):
         def step(i, carry):
-            c = lax.rem(start + i, chans)
+            c = far_first(i, chans, t, tm_count)
             ot, oj = owner_of(c)
             act(i, c, ot, oj)
             return carry
@@ -324,7 +330,7 @@
         def _():
             stage(i + early, 0)
 
-    over_channels(first, send_first)
+    over_channels(send_first)
 
     def own(p):
         @pl.when(active)
@@ -361,7 +367,7 @@
                 volt_copy(c, p - 1, ot, oj).wait_send()
                 volt_copy(c, p, ot, oj).start()
 
-        over_channels(first, send_next)
+        over_channels(send_next)
 
     for load in loads:
         load.wait()
@@ -405,10 +411,15 @@
                 power[d, odd * q : (odd + 1) * q] = summed[odd, d * q : (d + 1) * q]
 
         def send_power(i, carry):
-            power_copy(lax.rem(me + i, devices)).start()
-            return carry
-
-        lax.fori_loop(1, devices, send_power, 0)
+            d = far_first(i, devices, t, tm_count, j)
+
+            @pl.when(d != me)
+            def _():
+                power_copy(d).start()
+
+            return carry
+
+        lax.fori_loop(0, devices, send_power, 0)
         pltpu.make_async_copy(power.at[me], gathered.at[mine], power_recv).start()
 
     pltpu.make_async_copy(gathered, gathered, power_recv).wait()
@@ -435,7 +446,7 @@
             volt_copy(c, pols - 1, ot, oj).wait_send()
 
     over_column(wait_rows)
-    over_channels(first, wait_volt)
+    over_channels(wait_volt)
 
     @pl.when(active)
     def _():

time: 77.9 us -> 78.8 us (1.012); the launches traced: 76.5 us -> 78.6 us
  Pallas kernels: 75.1 us -> 77.2 us
    pallas_call x1, Pallas kernels: 75.1 us -> 77.2 us  [fused(): pl.pallas_call(functools.partial(fused_kernel, tm_count=tm_count, grp_cou...]
where the time goes in v6:
time: 78.8 us; the launch traced here: 78.6 us
  Pallas kernels  77.2 us (98%)
  local copies, waits for them, and re-layouts  1.47 us (2%)
    pallas_call x1, Pallas kernels, fused(): pl.pallas_call(functools.partial(fused_kernel, tm_count=tm_count, grp_cou...  77.2 us

profile of v6, /device:TPU:0, one launch (start us, length us, event | category | flops | bytes accessed | tf_op | source)
XLA Modules:
  0.0 78.6 jit_solution(13312808962960939974)
XLA Ops:
  0.0 77.2 %shard_map.100 = f32[4,4096]{1,0:T(4,128)} custom-call(s32[24]{0:T(128)} %shifts.1, s32[24]{0:T(128)} %group_of.1, bf16[24,2,2,8192]{3,2,1,0:T(2,128)(2,1)} %bitcast.2, f32[24,64,512]{2,1,0:T(8,128)} %chirp.1, bf16[2,1024,1024]{2,1,0:T(8,128)(2,1)} %constant.12.clone.h_left, bf16[2,2,512,512]{3,2,1,0:T(8,128)(2,1)} %constant.13.clone.h_ahead, ...), custom_call_target="tpu_custom_call" | custom-call | tf_op jit(solution)/shard_map/pallas_call | solution.py:470
  77.2 1.5 %copy.12 = f32[1,4,4096]{2,1,0:T(4,128)} copy(f32[1,4,4096]{2,1,0:T(4,128)} %bitcast.3) | data formatting | bytes 131072

commit v7 on v5

--- a/solution.py
+++ b/solution.py
@@ -279,13 +279,11 @@
         c = lax.rem(first + i, chans)
         staged[c, p] = raw[c, p].astype(f32).reshape(2, rows, f).astype(bf16)
 
-    def stage_early(i, carry):
-        stage(i, 0)
-        return carry
-
-    early = chans // 3
-    fetch.wait()
-    lax.fori_loop(0, early, stage_early, 0)
+    def code_rows(i, c):
+        load_rows(i, c).wait()
+        rows16[i] = jnp.round(rows32[i] * (32768.0 / math.pi)).astype(jnp.int32).astype(jnp.int16)
+
+    over_column(code_rows)
     pl.semaphore_wait(barrier, devices - 1)
 
     k_slot = pl.ds(pl.multiple_of(t * k_rows, k_rows), k_rows)
@@ -315,14 +313,25 @@
     def elsewhere(ot, oj):
         return (oj != j) | (ot != t)
 
+    def send_rows(i, c):
+        @pl.when(i != t)
+        def _():
+            chirp_copy(i).start()
+
+        @pl.when(i == t)
+        def _():
+            pltpu.make_async_copy(rows16.at[i], phase.at[k_slot], chirp_recv).start()
+
+    over_column(send_rows)
+
+    fetch.wait()
+
     def send_first(i, c, ot, oj):
+        stage(i, 0)
+
         @pl.when(elsewhere(ot, oj))
         def _():
             volt_copy(c, 0, ot, oj).start()
-
-        @pl.when(i + early < chans)
-        def _():
-            stage(i + early, 0)
 
     over_channels(first, send_first)
 
@@ -332,20 +341,6 @@
             pltpu.make_async_copy(staged.at[mine, p], z.at[p, :, z_slot], volt_recv.at[p]).start()
 
     own(0)
-
-    def send_rows(i, c):
-        load_rows(i, c).wait()
-        rows16[i] = jnp.round(rows32[i] * (32768.0 / math.pi)).astype(jnp.int32).astype(jnp.int16)
-
-        @pl.when(i != t)
-        def _():
-            chirp_copy(i).start()
-
-        @pl.when(i == t)
-        def _():
-            pltpu.make_async_copy(rows16.at[i], phase.at[k_slot], chirp_recv).start()
-
-    over_column(send_rows)
 
     for p in range(1, pols):
         def stage_next(i, carry):

time: 77.9 us -> 75.6 us (0.970); the launches traced: 76.5 us -> 75.3 us
  Pallas kernels: 75.1 us -> 73.9 us
    pallas_call x1, Pallas kernels: 75.1 us -> 73.9 us  [fused(): pl.pallas_call(functools.partial(fused_kernel, tm_count=tm_count, grp_cou...]
where the time goes in v7:
time: 75.6 us; the launch traced here: 75.3 us
  Pallas kernels  73.9 us (98%)
  local copies, waits for them, and re-layouts  1.47 us (2%)
    pallas_call x1, Pallas kernels, fused(): pl.pallas_call(functools.partial(fused_kernel, tm_count=tm_count, grp_cou...  73.9 us

profile of v7, /device:TPU:0, one launch (start us, length us, event | category | flops | bytes accessed | tf_op | source)
XLA Modules:
  0.0 75.3 jit_solution(386276767017871428)
XLA Ops:
  0.0 73.9 %shard_map.100 = f32[4,4096]{1,0:T(4,128)} custom-call(s32[24]{0:T(128)} %shifts.1, s32[24]{0:T(128)} %group_of.1, bf16[24,2,2,8192]{3,2,1,0:T(2,128)(2,1)} %bitcast.2, f32[24,64,512]{2,1,0:T(8,128)} %chirp.1, bf16[2,1024,1024]{2,1,0:T(8,128)(2,1)} %constant.12.clone.h_left, bf16[2,2,512,512]{3,2,1,0:T(8,128)(2,1)} %constant.13.clone.h_ahead, ...), custom_call_target="tpu_custom_call" | custom-call | tf_op jit(solution)/shard_map/pallas_call | solution.py:454
  73.9 1.5 %copy.12 = f32[1,4,4096]{2,1,0:T(4,128)} copy(f32[1,4,4096]{2,1,0:T(4,128)} %bitcast.3) | data formatting | bytes 131072
